TPU v7x, 128 devices: a whole 4x4x4 slice. The times are simulated.
128 devices in a mesh: seq: 4 (over x), fsdp: 16 (over z, y), dp: 2 (over core).
Axes of the slice: x: 4, y: 4, z: 4, core: 2. Of those that a mesh axis runs over, the one named last changes fastest.
Arguments:
- layer_input: bfloat16 [32, 1024, 8192], P(('fsdp', 'dp'), 'seq'), may hold values from -6 to 6
- c_weight: bfloat16 [8192, 512], P('fsdp'), may hold values from -0.0625 to 0.0625
- head_input: bfloat16 [32, 1024, 8192], P(('fsdp', 'dp'), 'seq'), may hold values from -6 to 6
- b_input: bfloat16 [32, 1024, 512], P(('fsdp', 'dp'), 'seq'), may hold values from -0.1796875 to 0.1796875
- log_decay: float32 [32, 64, 1024], P(('fsdp', 'dp'), None, 'seq'), may hold values from -1 to 0
- skip_gain: float32 [64], replicated, may hold values from 0.5 to 2
- out_grad: bfloat16 [32, 1024, 8192], P(('fsdp', 'dp'), 'seq'), may hold values from -0.29882812 to 0.29882812
Outputs:
- head_input_grad: bfloat16 [32, 1024, 8192], P(('fsdp', 'dp'), 'seq')
- b_input_grad: bfloat16 [32, 1024, 512], P(('fsdp', 'dp'), 'seq')
- c_weight_grad: float32 [8192, 512], P('fsdp')
- log_decay_grad: float32 [32, 64, 1024], P(('fsdp', 'dp'), None, 'seq')
- skip_gain_grad: float32 [64], replicated
All inputs are finite; a program needn't handle non-finite values.
Results may differ from a plain program's by a relative error of at most 0.027.
Values may be sent and summed in bfloat16 or wider, within the bound.
A program may use at most 192 MiB of HBM per device.

v0:
```python
import jax
import jax.numpy as jnp
from jax import lax
from jax.sharding import PartitionSpec as P

HEAD_COUNT = 64
P_SIZE = 128
N = 128
G = 4
BLK = 256
HG = 16


HIGHEST = lax.Precision.HIGHEST


def entering_2(array, axis, combine, identity, reverse):
    peers, index = (lax.axis_size(axis), lax.axis_index(axis))
    everything = jax.tree.map(
        lambda part, kind: lax.all_gather(part.astype(kind), axis),
        array,
        (jnp.bfloat16, jnp.bfloat16),
    )
    start = jax.tree.map(
        lambda part, zero: jnp.broadcast_to(jnp.asarray(zero, part.dtype), part.shape),
        array,
        identity,
    )

    def turn(k, before):
        at = peers - 1 - k if reverse else k
        reached = at > index if reverse else at < index
        new = combine(
            before, jax.tree.map(lambda part, own: part[at].astype(own.dtype), everything, array)
        )
        return jax.tree.map(lambda a, b: jnp.where(reached, a, b), new, before)

    return lax.fori_loop(0, peers, turn, start)


def block_forward(values, b_block, c_block, log_block, skip_gain, entering):
    length = values.shape[0]
    running = jnp.cumsum(log_block, axis=1)
    ending = running[:, -1]
    spread = running[:, :, None] - running[:, None, :]
    causal = jnp.arange(length)[:, None] >= jnp.arange(length)[None, :]
    decays = jnp.exp(jnp.where(causal[None], spread, -1e30))
    b_groups = b_block.reshape(length, G, N)
    c_groups = c_block.reshape(length, G, N)
    scores = jnp.einsum("tgn,sgn->gts", c_groups, b_groups, preferred_element_type=jnp.float32)
    mixing = (decays.reshape(G, HG, length, length) * scores[:, None]).astype(jnp.bfloat16)
    grouped = values.reshape(length, G, HG, P_SIZE)
    within = jnp.einsum("gkts,sgkp->tgkp", mixing, grouped, preferred_element_type=jnp.float32)
    from_start = jnp.exp(running).T.reshape(length, G, HG, 1)
    c_decayed = c_groups[:, :, None, :].astype(jnp.float32) * from_start
    carried = jnp.einsum(
        "tgkn,gkpn->tgkp", c_decayed, entering.reshape(G, HG, P_SIZE, N), precision=HIGHEST
    )
    to_end = jnp.exp(ending[None, :] - running.T).reshape(length, G, HG, 1)
    b_decayed = (b_groups[:, :, None, :].astype(jnp.float32) * to_end).astype(jnp.bfloat16)
    own_state = jnp.einsum(
        "sgkp,sgkn->gkpn", grouped, b_decayed, preferred_element_type=jnp.float32
    )
    leaving = jnp.exp(ending)[:, None, None] * entering + own_state.reshape(HEAD_COUNT, P_SIZE, N)
    output = (
        within + carried + skip_gain.reshape(G, HG)[None, :, :, None] * grouped.astype(jnp.float32)
    )
    return (output.reshape(length, HEAD_COUNT * P_SIZE).astype(jnp.bfloat16), leaving)


def span_forward(values, b_span, c_span, log_span, skip_gain, entering):
    blocks_here = values.shape[0] // BLK
    pieces = (
        values.reshape(blocks_here, BLK, HEAD_COUNT * P_SIZE),
        b_span.reshape(blocks_here, BLK, G * N),
        c_span.reshape(blocks_here, BLK, G * N),
        jnp.moveaxis(log_span.reshape(HEAD_COUNT, blocks_here, BLK), 1, 0),
    )

    def advance(states, block_in):
        out_block, leaving = block_forward(
            block_in[0], block_in[1], block_in[2], block_in[3], skip_gain, states
        )
        return (leaving, out_block)

    leaving, outputs = lax.scan(advance, entering, pieces)
    return (outputs.reshape(values.shape[0], HEAD_COUNT * P_SIZE), leaving)


def span_summary(values, b_span, log_span):
    length = values.shape[0]
    running = jnp.cumsum(log_span, axis=1)
    ending = running[:, -1]
    to_end = jnp.exp(ending[None, :] - running.T).reshape(length, G, HG, 1)
    b_decayed = (b_span.reshape(length, G, 1, N).astype(jnp.float32) * to_end).astype(jnp.bfloat16)
    own_state = jnp.einsum(
        "sgkp,sgkn->gkpn",
        values.reshape(length, G, HG, P_SIZE),
        b_decayed,
        preferred_element_type=jnp.float32,
    )
    return (jnp.exp(ending), own_state.reshape(HEAD_COUNT, P_SIZE, N))


def span_adjoint(grad_span, c_span, log_span):
    length = grad_span.shape[0]
    running = jnp.cumsum(log_span, axis=1)
    from_start = jnp.exp(running).T.reshape(length, G, HG, 1)
    c_decayed = (c_span.reshape(length, G, 1, N).astype(jnp.float32) * from_start).astype(
        jnp.bfloat16
    )
    adjoint = jnp.einsum(
        "tgkp,tgkn->gkpn",
        grad_span.reshape(length, G, HG, P_SIZE),
        c_decayed,
        preferred_element_type=jnp.float32,
    )
    return adjoint.reshape(HEAD_COUNT, P_SIZE, N)


def chain_link(earlier, later):
    product = earlier[0] * later[0]
    combined = later[0][:, None, None] * earlier[1] + later[1]
    return (product, combined)


def on_device(layer_input, c_weight, head_input, b_input, log_decay, skip_gain, out_grad):
    tok_rows = layer_input[0]
    columns = tok_rows
    c_span = jnp.dot(
        columns,
        lax.all_gather(c_weight, "fsdp", axis=0, tiled=True),
        preferred_element_type=jnp.float32,
    ).astype(jnp.bfloat16)
    values = head_input[0]
    b_span = b_input[0]
    log_span = log_decay[0]
    grad_span = out_grad[0]
    span_decay, own_state = span_summary(values, b_span, log_span)
    decay_wire = span_decay.astype(jnp.bfloat16).astype(jnp.float32)
    own_wire = own_state.astype(jnp.bfloat16).astype(jnp.float32)
    adjoint_wire = (
        span_adjoint(grad_span, c_span, log_span).astype(jnp.bfloat16).astype(jnp.float32)
    )
    identity = (
        jnp.ones((HEAD_COUNT,), jnp.float32),
        jnp.zeros((HEAD_COUNT, P_SIZE, N), jnp.float32),
    )
    entering = entering_2((decay_wire, own_wire), "seq", chain_link, identity, False)[1]
    leaving_grad = entering_2((decay_wire, adjoint_wire), "seq", chain_link, identity, True)[1]
    entering = lax.optimization_barrier(entering.astype(jnp.bfloat16)).astype(jnp.float32)
    leaving_grad = lax.optimization_barrier(leaving_grad.astype(jnp.bfloat16)).astype(jnp.float32)
    primal, pullback = jax.vjp(span_forward, values, b_span, c_span, log_span, skip_gain, entering)
    values_grad, b_grad, c_grad, log_grad, skip_part, enter_grad = pullback(
        (grad_span, leaving_grad)
    )
    columns = tok_rows
    grad_shard = lax.psum_scatter(
        lax.dot_general(
            columns, c_grad, (((0,), (0,)), ((), ())), preferred_element_type=jnp.float32
        ).astype(jnp.bfloat16),
        "fsdp",
        scatter_dimension=0,
        tiled=True,
    )
    weight_grad = lax.psum(grad_shard, ("seq", "dp")).astype(jnp.float32)
    documents = lax.axis_size("fsdp") * lax.axis_size("dp")
    skip_total = lax.psum(skip_part, ("seq", "fsdp", "dp"))
    return (
        values_grad[None],
        b_grad[None],
        weight_grad / documents,
        log_grad[None],
        skip_total / documents,
    )


def solution(mesh):
    in_specs = (
        P(("fsdp", "dp"), "seq", None),
        P("fsdp", None),
        P(("fsdp", "dp"), "seq", None),
        P(("fsdp", "dp"), "seq", None),
        P(("fsdp", "dp"), None, "seq"),
        P(),
        P(("fsdp", "dp"), "seq", None),
    )
    out_specs = (
        P(("fsdp", "dp"), "seq", None),
        P(("fsdp", "dp"), "seq", None),
        P("fsdp", None),
        P(("fsdp", "dp"), None, "seq"),
        P(),
    )
    return jax.shard_map(
        on_device, mesh=mesh, in_specs=in_specs, out_specs=out_specs, check_vma=False
    )
```

profile of v0, /device:TPU:1, one launch (start us, length us, event | category | flops | bytes accessed | tf_op | source)
XLA Modules:
  0.0 421.1 jit_solution(13188554458518510789)
XLA Ops:
  14.8 4.8 %fusion.40 = bf16[4,16,128,128]{3,2,1,0:T(8,128)(2,1)S(1)} fusion(bf16[256,4,16,128]{3,2,1,0:T(8,128)(2,1)S(1)} %bitcast.145, f32[256,4,16]{0,2,1:T(8,128)S(1)} %bitcast.158, f32[256,4,128]{0,2,1:T(8,128)S(1)} %convert_element_type.256), kind=kOutput, calls=%fused_computation.57 | convolution fusion | flops 542113792 | bytes 6881280 | tf_op jit(solution)/shard_map/sgkp,sgkn->gkpn/dot_general | solution.py:96
  22.7 6.4 %copy.144 = bf16[1,256,8192]{1,2,0:T(8,128)(2,1)} copy(bf16[1,256,8192]{2,1,0:T(8,128)(2,1)} %param.17) | data formatting | bytes 8388608 | tf_op args[6]
  29.2 55.1 %all-gather.5.cloned.1.call-done = bf16[8192,512]{1,0:T(8,128)(2,1)} async-done(((bf16[512,512]{1,0:T(8,128)(2,1)}), bf16[8192,512]{1,0:T(8,128)(2,1)}) %all-gather.5.cloned.1.call-update) | async-done | bytes 8388624 | tf_op jit(solution)/shard_map/all_gather | solution.py:132
  84.3 7.0 %fusion.43 = bf16[256,512]{1,0:T(8,128)(2,1)S(1)} fusion(bf16[8192,512]{1,0:T(8,128)(2,1)} %all-gather.5.cloned.1.call-done, bf16[1,256,8192]{2,1,0:T(8,128)(2,1)} %param.11), kind=kOutput, calls=%fused_computation.60 | convolution fusion | flops 2147614720 | bytes 12845056 | tf_op jit(solution)/shard_map/dot_general | solution.py:130
  100.2 9.5 %all-reduce.1 = bf16[256]{0:T(256)(128)(2,1)S(1)} all-reduce(bf16[256]{0:T(256)(128)(2,1)S(1)} %dynamic-update-slice), channel_id=2, replica_groups=mesh['seq'=4,'fsdp'=16,'dp'=2] {'seq'}, use_global_device_ids=true, to_apply=%add.1 | all-reduce | flops 256 | bytes 1024
  110.5 58.3 %all-gather.9.cloned.1.call-done = bf16[4,64,128,128]{3,2,1,0:T(8,128)(2,1)} async-done(((bf16[1,64,128,128]{3,2,1,0:T(8,128)(2,1)}), bf16[4,64,128,128]{3,2,1,0:T(8,128)(2,1)}) %all-gather.9.cloned.1.call-update) | async-done | bytes 8388624 | tf_op jit(solution)/shard_map/all_gather | solution.py:20
  168.8 23.4 %while.21 = (s32[]{:T(128)}, f32[64,128,128]{2,1,0:T(8,128)}, s32[]{:T(128)}, bf16[4,64]{1,0:T(4,128)(2,1)S(1)}, bf16[4,64,128,128]{3,2,1,0:T(8,128)(2,1)}, /*index=5*/s32[]{:T(128)}, s32[]{:T(128)}) while((s32[]{:T(128)}, f32[64,128,128]{2,1,0:T(8,128)}, s32[]{:T(128)}, bf16[4,64]{1,0:T(4,128)(2,1)S(1)}, ...), condition=%wide.region_7.8_spmd.clone, body=%wide.region_6.7_spmd.clone.sunk | while | flops 5242948 | bytes 10486513 | solution.py:38
  173.4 5.9 %fusion.74 = f32[64,128,128]{2,1,0:T(8,128)} fusion(f32[64,128,128]{2,1,0:T(8,128)} %get-tuple-element.601, bf16[4,64,128,128]{3,2,1,0:T(8,128)(2,1)} %get-tuple-element.611, s32[]{:T(128)S(6)} %copy.210, f32[64]{0:T(128)S(1)} %bitcast_convert_fusion.5, pred[]{:T(512)S(6)} %compare.8, pred[]{:T(512)S(6)} %lt.47), kind=kLoop, calls=%fused_computation.4.clone.1 | loop fusion | flops 5242880 | bytes 10486022 | tf_op jit(solution)/shard_map/while/body/eval_jaxpr/jit(_where)/select_n | solution.py:36
  179.3 6.7 %fusion.74 = f32[64,128,128]{2,1,0:T(8,128)} fusion(f32[64,128,128]{2,1,0:T(8,128)} %get-tuple-element.601, bf16[4,64,128,128]{3,2,1,0:T(8,128)(2,1)} %get-tuple-element.611, s32[]{:T(128)S(6)} %copy.210, f32[64]{0:T(128)S(1)} %bitcast_convert_fusion.5, pred[]{:T(512)S(6)} %compare.8, pred[]{:T(512)S(6)} %lt.47), kind=kLoop, calls=%fused_computation.4.clone.1 | loop fusion | flops 5242880 | bytes 10486022 | tf_op jit(solution)/shard_map/while/body/eval_jaxpr/jit(_where)/select_n | solution.py:36
  186.1 6.1 %fusion.74 = f32[64,128,128]{2,1,0:T(8,128)} fusion(f32[64,128,128]{2,1,0:T(8,128)} %get-tuple-element.601, bf16[4,64,128,128]{3,2,1,0:T(8,128)(2,1)} %get-tuple-element.611, s32[]{:T(128)S(6)} %copy.210, f32[64]{0:T(128)S(1)} %bitcast_convert_fusion.5, pred[]{:T(512)S(6)} %compare.8, pred[]{:T(512)S(6)} %lt.47), kind=kLoop, calls=%fused_computation.4.clone.1 | loop fusion | flops 5242880 | bytes 10486022 | tf_op jit(solution)/shard_map/while/body/eval_jaxpr/jit(_where)/select_n | solution.py:36
  195.4 5.0 %fusion.10 = (f32[256,4,16]{0,2,1:T(8,128)}, bf16[256,4,128]{0,2,1:T(8,128)(2,1)S(1)}) fusion(f32[256,4,128]{0,2,1:T(8,128)S(1)} %copy.148, f32[256,4,16]{0,2,1:T(8,128)} %bitcast.162, bf16[4,16,128,128]{3,2,1,0:T(8,128)(2,1)S(1)} %bitcast.134, bf16[4,16,128,256]{3,2,1,0:T(8,128)(2,1)} %bitcast.141), kind=kOutput, calls=%fused_computation.21 | convolution fusion | flops 545112064 | bytes 7208960 | tf_op jit(solution)/shard_map/transpose(jvp())/while/body/eval_jaxpr/tgkn,gkpn->tgkp/dot_general | solution.py:56
  200.6 18.1 %fusion.6 = (f32[4,16,256]{2,1,0:T(8,128)}, f32[4,16,256]{2,1,0:T(8,128)}, bf16[4,256,256]{2,1,0:T(8,128)(2,1)S(1)}) fusion(f32[4,256,256]{2,1,0:T(8,128)S(1)} %fusion.55, f32[4,16,256]{2,1,0:T(8,128)S(1)} %copy-done.17, pred[256,256]{1,0:T(8,128)(4,1)S(1)} %copy-done.19, bf16[4,16,128,256]{3,2,1,0:T(8,128)(2,1)S(1)} %bitcast.144, ...), kind=kOutput, calls=%fused_computation.14 | convolution fusion | flops 1119584256 | bytes 10223616 | tf_op jit(solution)/shard_map/transpose(jvp())/while/body/eval_jaxpr/gkts,sgkp->tgkp/dot_general | solution.py:53
  219.0 5.6 %fusion.7 = bf16[8192,512]{0,1:T(8,128)(2,1)} fusion(bf16[256,512]{0,1:T(8,128)(2,1)S(1)} %bitcast.153, bf16[1,256,8192]{2,1,0:T(8,128)(2,1)S(1)} %copy-done.1), kind=kOutput, calls=%fused_computation.16 | convolution fusion | flops 2151677952 | bytes 12845056 | tf_op jit(solution)/shard_map/dot_general | solution.py:159
  225.3 5.0 %multiply_reduce_fusion = f32[8192]{0:T(1024)S(1)} fusion(bf16[1,256,8192]{2,1,0:T(8,128)(2,1)} %param.13, bf16[1,256,8192]{2,1,0:T(8,128)(2,1)} %param.17), kind=kLoop, calls=%fused_computation.26 | loop fusion | flops 8380416 | bytes 8421376 | tf_op jit(solution)/shard_map/transpose(jvp())/while/body/eval_jaxpr/reduce_sum | solution.py:66
  230.5 66.9 %psum.15 = f32[64]{0:T(128)S(1)} all-reduce(f32[64]{0:T(128)S(1)} %reshape.375), channel_id=1, replica_groups=mesh['seq'=4,'fsdp'=16,'dp'=2] {'seq','fsdp','dp'}, use_global_device_ids=true, to_apply=%region_21.22 | all-reduce | flops 64 | bytes 512 | tf_op jit(solution)/shard_map/psum | solution.py:168
  300.2 7.3 %fusion.8 = bf16[4,16,256,128]{2,3,1,0:T(8,128)(2,1)} fusion(bf16[4,16,128,256]{3,2,1,0:T(8,128)(2,1)} %bitcast.142, f32[4,256,256]{2,1,0:T(8,128)} %copy-done.6, f32[4,16,256]{2,1,0:T(8,128)S(1)} %copy-done.18, pred[256,256]{1,0:T(8,128)(4,1)S(1)} %copy-done.20), kind=kOutput, calls=%fused_computation.17 | convolution fusion | flops 1090519040 | bytes 9568256 | tf_op jit(solution)/shard_map/transpose(jvp())/while/body/eval_jaxpr/gkts,sgkp->tgkp/dot_general | solution.py:53
  307.5 22.6 %while.20 = (s32[]{:T(128)}, f32[64,128,128]{2,1,0:T(8,128)}, s32[]{:T(128)}, bf16[4,64]{1,0:T(4,128)(2,1)S(1)}, bf16[4,64,128,128]{3,2,1,0:T(8,128)(2,1)}, /*index=5*/s32[]{:T(128)}, s32[]{:T(128)}, s32[]{:T(128)}, s32[]{:T(128)}) while((s32[]{:T(128)}, f32[64,128,128]{2,1,0:T(8,128)}, s32[]{:T(128)}, ...), condition=%wide.region_3.4_spmd.clone, body=%wide.region_2.3_spmd.clone.sunk | while | flops 5242952 | bytes 10486575 | solution.py:38
  312.2 6.0 %fusion.73 = f32[64,128,128]{2,1,0:T(8,128)} fusion(f32[64,128,128]{2,1,0:T(8,128)} %get-tuple-element.576, bf16[4,64,128,128]{3,2,1,0:T(8,128)(2,1)} %get-tuple-element.588, s32[]{:T(128)S(6)} %select_n.103, f32[64]{0:T(128)S(1)} %bitcast_convert_fusion.4, pred[]{:T(512)S(6)} %compare.7, pred[]{:T(512)S(6)} %gt.12), kind=kLoop, calls=%fused_computation.1.clone.1 | loop fusion | flops 5242880 | bytes 10486022 | tf_op jit(solution)/shard_map/while/body/eval_jaxpr/jit(_where)/select_n | solution.py:36
  318.3 5.9 %fusion.73 = f32[64,128,128]{2,1,0:T(8,128)} fusion(f32[64,128,128]{2,1,0:T(8,128)} %get-tuple-element.576, bf16[4,64,128,128]{3,2,1,0:T(8,128)(2,1)} %get-tuple-element.588, s32[]{:T(128)S(6)} %select_n.103, f32[64]{0:T(128)S(1)} %bitcast_convert_fusion.4, pred[]{:T(512)S(6)} %compare.7, pred[]{:T(512)S(6)} %gt.12), kind=kLoop, calls=%fused_computation.1.clone.1 | loop fusion | flops 5242880 | bytes 10486022 | tf_op jit(solution)/shard_map/while/body/eval_jaxpr/jit(_where)/select_n | solution.py:36
  324.2 5.9 %fusion.73 = f32[64,128,128]{2,1,0:T(8,128)} fusion(f32[64,128,128]{2,1,0:T(8,128)} %get-tuple-element.576, bf16[4,64,128,128]{3,2,1,0:T(8,128)(2,1)} %get-tuple-element.588, s32[]{:T(128)S(6)} %select_n.103, f32[64]{0:T(128)S(1)} %bitcast_convert_fusion.4, pred[]{:T(512)S(6)} %compare.7, pred[]{:T(512)S(6)} %gt.12), kind=kLoop, calls=%fused_computation.1.clone.1 | loop fusion | flops 5242880 | bytes 10486022 | tf_op jit(solution)/shard_map/while/body/eval_jaxpr/jit(_where)/select_n | solution.py:36
  333.7 6.1 %fusion.12 = (f32[256,4,16]{0,2,1:T(8,128)}, bf16[256,4,128]{0,2,1:T(8,128)(2,1)}) fusion(f32[256,4,128]{0,2,1:T(8,128)S(1)} %copy-done.8, f32[256,4,16]{0,2,1:T(8,128)S(1)} %bitcast.160, bf16[4,16,128,128]{3,2,1,0:T(8,128)(2,1)S(1)} %bitcast.135, bf16[256,4,16,128]{3,2,1,0:T(8,128)(2,1)S(1)} %bitcast.147), kind=kOutput, calls=%fused_computation.25 | convolution fusion | flops 549306368 | bytes 7208960 | tf_op jit(solution)/shard_map/transpose(jvp())/while/body/eval_jaxpr/sgkp,sgkn->gkpn/dot_general | solution.py:61
  347.1 8.7 %fusion.21 = bf16[256,4,16,128]{0,3,2,1:T(8,128)(2,1)} fusion(bf16[256,4,16,128]{0,3,2,1:T(8,128)(2,1)} %bitcast.143, bf16[4,16,256,128]{2,3,1,0:T(8,128)(2,1)} %fusion.8, f32[4,16]{1,0:T(4,128)S(1)} %mul.237, bf16[4,16,128,128]{3,2,1,0:T(8,128)(2,1)} %bitcast.136, f32[256,4,16]{0,2,1:T(8,128)} %bitcast.159, f32[256,4,128]{0,2,1:T(8,128)} %copy-done.7), kind=kOutput, calls=%fused_computation.39 | convolution fusion | flops 553648128 | bytes 15270144 | tf_op jit(solution)/shard_map/transpose(jvp())/while/body/eval_jaxpr/sgkp,sgkn->gkpn/dot_general | solution.py:61
  356.0 6.3 %copy.175 = bf16[1,256,8192]{2,1,0:T(8,128)(2,1)} copy(bf16[1,256,8192]{1,2,0:T(8,128)(2,1)} %bitcast.148) | data formatting | bytes 8388608
  364.0 48.1 %all-reduce.4.cloned.1.call-done = bf16[512,512]{0,1:T(8,128)(2,1)} async-done(((bf16[512,512]{0,1:T(8,128)(2,1)}), bf16[512,512]{0,1:T(8,128)(2,1)}) %all-reduce.4.cloned.1.call-update) | async-done | bytes 524304 | tf_op jit(solution)/shard_map/psum | solution.py:166
  (129 shorter events, 51.4 us)
Async XLA Ops:
  7.2 77.1 %all-gather.5.cloned.1.call-start = ((), (), s32[]{:S(2)}) async-start(), calls=%async_computation.1 | async-start | bytes 8912896 | tf_op jit(solution)/shard_map/all_gather | solution.py:132
  7.9 160.9 %all-gather.9.cloned.1.call-start = ((), (), s32[]{:S(2)}) async-start(), calls=%async_computation.3 | async-start | bytes 10485760 | tf_op jit(solution)/shard_map/all_gather | solution.py:20
  11.1 3.7 copy-start.12
  11.2 3.6 copy-start.7
  14.7 4.9 %copy-start.3 = (bf16[32,8,64,128]{3,2,1,0:T(8,128)(2,1)}, bf16[32,8,64,128]{3,2,1,0:T(8,128)(2,1)S(1)}, u32[]{:S(2)}) copy-start(bf16[32,8,64,128]{3,2,1,0:T(8,128)(2,1)S(1)} %copy.186) | copy-start | bytes 12582916
  22.6 284.9 %all-gather.7.cloned.1.call-start = ((), (), s32[]{:S(2)}) async-start(), calls=%async_computation.2 | async-start | bytes 10485760 | tf_op jit(solution)/shard_map/all_gather | solution.py:20
  29.2 62.3 %copy-start.14 = (f32[256,64]{0,1:T(8,128)}, f32[256,64]{0,1:T(8,128)S(1)}, u32[]{:S(2)}) copy-start(f32[256,64]{0,1:T(8,128)S(1)} %copy.150) | copy-start | bytes 196612
  95.0 3.8 copy-start.23
  97.9 257.9 %reduce-scatter.2.cloned.1.call-start = ((), (), s32[]{:S(2)}) async-start(), calls=%async_computation.4 | async-start | bytes 8912896 | tf_op jit(solution)/shard_map/reduce_scatter | solution.py:158
  195.3 5.1 %copy-start.6 = (f32[4,256,256]{2,1,0:T(8,128)}, f32[4,256,256]{2,1,0:T(8,128)S(1)}, u32[]{:S(2)}) copy-start(f32[4,256,256]{2,1,0:T(8,128)S(1)} %fusion.55) | copy-start | bytes 3145732
  195.4 5.1 %copy-start.2 = (bf16[1,256,8192]{1,2,0:T(8,128)(2,1)S(1)}, bf16[1,256,8192]{1,2,0:T(8,128)(2,1)}, u32[]{:S(2)}) copy-start(bf16[1,256,8192]{1,2,0:T(8,128)(2,1)} %copy.144) | copy-start | bytes 12582916
  195.4 5.2 %copy-start.4 = (bf16[32,8,64,128]{3,2,1,0:T(8,128)(2,1)S(1)}, bf16[32,8,64,128]{3,2,1,0:T(8,128)(2,1)}, u32[]{:S(2)}) copy-start(bf16[32,8,64,128]{3,2,1,0:T(8,128)(2,1)} %copy-done.3) | copy-start | bytes 12582916
  195.4 5.2 %copy-start.17 = (f32[4,16,256]{2,1,0:T(8,128)S(1)}, f32[4,16,256]{2,1,0:T(8,128)}, u32[]{:S(2)}) copy-start(f32[4,16,256]{2,1,0:T(8,128)} %reduce_window_sum.59) | copy-start | bytes 196612
  195.4 5.2 %copy-start.19 = (pred[256,256]{1,0:T(8,128)(4,1)S(1)}, pred[256,256]{1,0:T(8,128)(4,1)}, u32[]{:S(2)}) copy-start(pred[256,256]{1,0:T(8,128)(4,1)} %iota_compare_fusion) | copy-start | bytes 196612
  200.6 18.4 %copy-start.1 = (bf16[1,256,8192]{2,1,0:T(8,128)(2,1)S(1)}, bf16[1,256,8192]{2,1,0:T(8,128)(2,1)}, u32[]{:S(2)}) copy-start(bf16[1,256,8192]{2,1,0:T(8,128)(2,1)} %param.11) | copy-start | bytes 12582916
  224.6 187.5 %all-reduce.4.cloned.1.call-start = ((), (), s32[]{:S(2)}) async-start(), calls=%async_computation.5 | async-start | bytes 1048576 | tf_op jit(solution)/shard_map/psum | solution.py:166
  225.3 72.6 %copy-start.16 = (f32[4,16,256]{2,1,0:T(8,128)S(1)}, f32[4,16,256]{2,1,0:T(8,128)}, u32[]{:S(2)}) copy-start(f32[4,16,256]{2,1,0:T(8,128)} %get-tuple-element.474) | copy-start | bytes 196612
  225.3 73.4 %copy-start.21 = (f32[4,16,256]{2,1,0:T(8,128)S(1)}, f32[4,16,256]{2,1,0:T(8,128)}, u32[]{:S(2)}) copy-start(f32[4,16,256]{2,1,0:T(8,128)} %get-tuple-element.473) | copy-start | bytes 196612
  225.3 74.1 %copy-start.15 = (f32[256,4,16]{0,2,1:T(8,128)S(1)}, f32[256,4,16]{0,2,1:T(8,128)}, u32[]{:S(2)}) copy-start(f32[256,4,16]{0,2,1:T(8,128)} %get-tuple-element.476) | copy-start | bytes 196612
  225.3 74.9 %copy-start.18 = (f32[4,16,256]{2,1,0:T(8,128)S(1)}, f32[4,16,256]{2,1,0:T(8,128)}, u32[]{:S(2)}) copy-start(f32[4,16,256]{2,1,0:T(8,128)} %reduce_window_sum.59) | copy-start | bytes 196612
  225.3 74.9 %copy-start.20 = (pred[256,256]{1,0:T(8,128)(4,1)S(1)}, pred[256,256]{1,0:T(8,128)(4,1)}, u32[]{:S(2)}) copy-start(pred[256,256]{1,0:T(8,128)(4,1)} %iota_compare_fusion) | copy-start | bytes 196612
  330.1 3.6 copy-start.8
  330.1 3.6 copy-start.13
  332.8 6.9 %copy-start = (bf16[64,128,128]{2,1,0:T(8,128)(2,1)}, bf16[64,128,128]{2,1,0:T(8,128)(2,1)S(1)}, u32[]{:S(2)}) copy-start(bf16[64,128,128]{2,1,0:T(8,128)(2,1)S(1)} %convert_element_type.255) | copy-start | bytes 6291460
  (5 other events, 14.6 us)
Sparse Core Ops, SparseCore 0:
  10.1 74.0 all-gather.4
  85.9 82.7 all-gather.8
  170.4 84.6 all-gather.6
  258.4 85.3 reduce-scatter.1
  356.0 56.0 all-reduce.3
where the time goes:
time: 423 us; the launch traced here: 421 us
  waiting for transfers between devices  162 us (38%)
  blocking collectives  76.4 us (18%)
  matrix products  67.9 us (16%)
  other arithmetic  64.7 us (15%)
  local copies, waits for them, and re-layouts  34.8 us (8%)
  between operations  14.9 us (4%)
    psum x1, blocking collectives, on_device(): skip_total = lax.psum(skip_part, ('seq', 'fsdp', 'dp'))  66.9 us
    all_gather x2, waiting for transfers between devices, entering_2(): lax.all_gather(part.astype(kind), axis)  58.3 us
    all_gather x1, waiting for transfers between devices, on_device(): lax.all_gather(c_weight, 'fsdp', axis=0, tiled=True)  55.1 us
    psum x1, waiting for transfers between devices, on_device(): weight_grad = lax.psum(grad_shard, ('seq', 'dp')).astype(jnp.float32)  48.1 us
    select_n x8, other arithmetic, turn(): return jax.tree.map(lambda a, b: jnp.where(reached, a, b), new, before)  46 us
    dot_general x2, matrix products, block_forward(): jnp.einsum('gkts,sgkp->tgkp', mixing, grouped, preferred_element_type=jnp...  25.4 us
    unnamed x56, local copies, waits for them, and re-layouts  21 us
    dot_general x2, matrix products, block_forward(): jnp.einsum('sgkp,sgkn->gkpn', grouped, b_decayed, preferred_element_type=...  14.8 us
  transfers between devices with their start and end apart: 5, of which 3 were waited for; matrix products, arithmetic and copies ran while one was open for 39% of the time, Pallas kernels for 0%

commit v1 on v0

v1 whole, which is shorter than its diff:
```python
import jax
import jax.numpy as jnp
from jax import lax
from jax.experimental import pallas as pl
from jax.experimental.pallas import tpu as pltpu
from jax.sharding import PartitionSpec as P

HEADS = 64
GROUPS = 4
TOK = 256
HALF = 128
DIM = 8192
CH = 4
K = HEADS // CH
CW = CH * 128
OFF = 3
STEPS = 24
BF = jnp.bfloat16
F32 = jnp.float32
MESH = pl.DeviceIdType.MESH
HIGHEST = lax.Precision.HIGHEST
NT = (((1,), (1,)), ((), ()))


def dot(a, b):
    return jnp.dot(a, b, preferred_element_type=F32)


def dot_nt(a, b):
    return lax.dot_general(a, b, NT, preferred_element_type=F32)


def expand(columns):
    rows = columns.shape[0]
    return jnp.concatenate(
        [jnp.broadcast_to(columns[:, j : j + 1], (rows, 128)) for j in range(CH)], axis=1
    )


def kernel(
    li_hbm,
    cw_hbm,
    x_hbm,
    b_ref,
    log_ref,
    skip_ref,
    g_hbm,
    dx_hbm,
    db_ref,
    dw_ref,
    dlog_ref,
    dskip_ref,
    xs,
    gs,
    g3,
    x3,
    gp,
    gx2,
    li,
    w,
    er,
    own,
    lr,
    adj,
    red,
    t1,
    u1,
    t2,
    u2,
    logp,
    cum,
    fac,
    skg,
    b4,
    bt,
    cb,
    ct,
    smat,
    stmat,
    cp_own,
    cp_send,
    cp_recv,
    ds_acc,
    dc_acc,
    db_acc,
    cg,
    acc,
    xr,
    fin,
    sk,
    load_x,
    load_g,
    load_li,
    load_w,
    store_x,
    li_send,
    li_recv,
    w_send,
    w_recv,
    f_send,
    f_recv,
    b_send,
    b_recv,
    cp_ssem,
    cp_rsem,
    cg_send,
    cg_recv,
    r_send,
    r_recv,
    x_send,
    x_recv,
    a_send,
    a_recv,
    p_send,
    p_recv,
    sk_send,
    sk_recv,
):
    s = lax.axis_index("seq")
    fs = lax.axis_index("fsdp")
    c = lax.axis_index("dp")
    z, y = lax.div(fs, 4), lax.rem(fs, 4)

    def at(seq=None, zz=None, yy=None, core=None):
        seq = s if seq is None else seq
        zz = z if zz is None else zz
        yy = y if yy is None else yy
        core = c if core is None else core
        return {"seq": seq, "fsdp": zz * 4 + yy, "dp": core}

    def plus(i, n):
        return lax.rem(i + n, 4)

    def remote(src, dst, send, recv, device):
        return pltpu.make_async_remote_copy(
            src_ref=src,
            dst_ref=dst,
            send_sem=send,
            recv_sem=recv,
            device_id=device,
            device_id_type=MESH,
        )

    sibling = at(core=1 - c)

    def lanes(k):
        return pl.ds(pl.multiple_of(k * CW, CW), CW)

    def get_x(k):
        return pltpu.make_async_copy(x_hbm.at[:, lanes(k)], xs.at[k], load_x.at[k])

    def get_g(k):
        return pltpu.make_async_copy(g_hbm.at[:, lanes(k)], gs.at[k], load_g.at[k])

    def put_x(k):
        return pltpu.make_async_copy(xs.at[k], dx_hbm.at[:, lanes(k)], store_x.at[k])

    def get_w(q):
        return pltpu.make_async_copy(
            cw_hbm.at[pl.ds(pl.multiple_of(c * 256, 256), 256), pl.ds(q * 256, 256)],
            w.at[q, z, y],
            load_w.at[q],
        )

    def li_lanes(k, core):
        return pl.ds(pl.multiple_of(k * 512 + core * 256, 256), 256)

    def li_slot(slot, k):
        return li.at[slot, :, pl.ds(pl.multiple_of(k * 256, 256), 256)]

    def fwd(k):
        return remote(own.at[k], er.at[k], f_send.at[k], f_recv.at[k], at(seq=plus(s, 1)))

    def bwd(k):
        return remote(adj.at[k], lr.at[k], b_send.at[k], b_recv.at[k], at(seq=plus(s, 3)))

    def toward(axis, d):
        if axis == 0:
            return at(zz=plus(z, 1 if d == 0 else 3))
        return at(yy=plus(y, 1 if d == 0 else 3))

    def w_copy(q, p, stage, d):
        phase, second = stage // 2, stage % 2
        axis = (1 - p) if phase == 0 else p
        me = z if axis == 0 else y
        idx = me if second == 0 else plus(me, 3 if d == 0 else 1)
        rows = pl.ds(p * 128, 128) if second == 0 else pl.ds(p * 128 + d * 64, 64)
        if phase == 0:
            ref = w.at[q, idx, y, rows] if axis == 0 else w.at[q, z, idx, rows]
        else:
            ref = w.at[q, idx, :, rows] if axis == 0 else w.at[q, :, idx, rows]
        return remote(
            ref, ref, w_send.at[q, p, stage, d], w_recv.at[q, p, stage, d], toward(axis, d)
        )

    def w_start(q, stage):
        for p in range(2):
            for d in range(2):
                w_copy(q, p, stage, d).start()

    def w_wait(q, stage):
        for p in range(2):
            for d in range(2):
                w_copy(q, p, stage, d).wait_recv()

    def cp_copy(q):
        return remote(cp_send.at[q], cp_recv.at[q], cp_ssem.at[q], cp_rsem.at[q], sibling)

    def cg_copy(g):
        return remote(cg.at[0, g], cg.at[1, g], cg_send.at[g], cg_recv.at[g], sibling)

    def r_axis(p, phase):
        return p if phase == 0 else 1 - p

    def r_ref(g, p, phase, idx, rows):
        if phase == 0:
            return red.at[g, idx, :, rows] if p == 0 else red.at[g, :, idx, rows]
        return red.at[g, z, idx, rows] if p == 0 else red.at[g, idx, y, rows]

    def r_full(p):
        return pl.ds(p * 64, 64)

    def r_half(p, h):
        return pl.ds(p * 64 + h * 32, 32)

    def r_copy(g, p, stage, d):
        phase, second = stage // 2, stage % 2
        axis = r_axis(p, phase)
        me = z if axis == 0 else y
        if second == 0:
            src = r_ref(g, p, phase, plus(me, 2), r_half(p, d))
            dst = (t1 if phase == 0 else t2).at[g, p, d]
        else:
            src = r_ref(g, p, phase, plus(me, 1 if d == 0 else 3), r_full(p))
            dst = (u1 if phase == 0 else u2).at[g, p, d]
        return remote(
            src, dst, r_send.at[g, p, stage, d], r_recv.at[g, p, stage, d], toward(axis, d)
        )

    def r_start(g, stage):
        for p in range(2):
            for d in range(2):
                r_copy(g, p, stage, d).start()

    def r_middle(g, phase):
        for p in range(2):
            me = z if r_axis(p, phase) == 0 else y
            for d in range(2):
                r_copy(g, p, 2 * phase, d).wait_recv()
                ref = r_ref(g, p, phase, plus(me, 1 if d == 0 else 3), r_half(p, d))
                got = (t1 if phase == 0 else t2)[g, p, d]
                ref[...] = (ref[...].astype(F32) + got.astype(F32)).astype(BF)
                r_copy(g, p, 2 * phase + 1, d).start()

    def r_last(g, phase):
        for p in range(2):
            me = z if r_axis(p, phase) == 0 else y
            buf = u1 if phase == 0 else u2
            for d in range(2):
                r_copy(g, p, 2 * phase + 1, d).wait_recv()
            ref = r_ref(g, p, phase, me, r_full(p))
            total = ref[...].astype(F32) + buf[g, p, 0].astype(F32) + buf[g, p, 1].astype(F32)
            ref[...] = total.astype(BF)

    def x_copy(n):
        to = plus(s, n)
        return remote(red.at[to, z, y], xr.at[n - 1], x_send.at[n], x_recv.at[n], at(seq=to))

    def a_copy(n):
        to = plus(s, n)
        return remote(fin.at[c, s], fin.at[c, s], a_send.at[n], a_recv.at[n], at(seq=to))

    def p_copy():
        return remote(fin.at[c], fin.at[c], p_send, p_recv, sibling)

    def sk_copy(axis, n):
        if axis == 3:
            return remote(sk.at[3, 0], sk.at[3, 1], sk_send.at[3, 1], sk_recv.at[3, 1], sibling)
        to = (
            at(zz=plus(z, n))
            if axis == 0
            else (at(yy=plus(y, n)) if axis == 1 else at(seq=plus(s, n)))
        )
        return remote(sk.at[axis, 0], sk.at[axis, n], sk_send.at[axis, n], sk_recv.at[axis, n], to)

    def sk_range(axis):
        return range(1, 2) if axis == 3 else range(1, 4)

    get_w(0).start()
    get_w(1).start()

    def load(k, _):
        get_x(k).start()
        return _

    lax.fori_loop(0, K, load, 0)

    def load_more(k, _):
        get_g(k).start()
        return _

    lax.fori_loop(0, K, load_more, 0)

    barrier = pltpu.get_barrier_semaphore()
    peers = [sibling]
    for n in range(1, 4):
        peers += [at(seq=plus(s, n)), at(zz=plus(z, n)), at(yy=plus(y, n))]
    for peer in peers:
        pl.semaphore_signal(barrier, inc=1, device_id=peer, device_id_type=MESH)
    pl.semaphore_wait(barrier, len(peers))

    get_w(0).wait()
    w_start(0, 0)

    def load_part(k, _):
        pltpu.make_async_copy(li_hbm.at[:, li_lanes(k, c)], li_slot(0, k), load_li).start()
        remote(li_hbm.at[:, li_lanes(k, 1 - c)], li_slot(1, k), li_send, li_recv, sibling).start()
        return _

    lax.fori_loop(0, 16, load_part, 0)

    rows_i = lax.broadcasted_iota(jnp.int32, (TOK, TOK), 0)
    cols_i = lax.broadcasted_iota(jnp.int32, (TOK, TOK), 1)
    tri = jnp.where(cols_i <= rows_i, 1.0, 0.0).astype(F32)
    low = rows_i[:HALF, :HALF] >= cols_i[:HALF, :HALF]
    lane = lax.broadcasted_iota(jnp.int32, (TOK, 128), 1)
    row = lax.broadcasted_iota(jnp.int32, (TOK, 128), 0)

    logp[...] = jnp.zeros_like(logp)
    logp[:HEADS] = log_ref[...]
    running = lax.dot_general(tri, logp[...], NT, precision=HIGHEST, preferred_element_type=F32)
    cum[...] = running
    ending = running[TOK - 1 : TOK]
    middle = jnp.where(row < HALF, running[HALF // 2 - 1 : HALF // 2], running[HALF + HALF // 2 - 1 : HALF + HALF // 2])
    edge = running[HALF - 1 : HALF]
    fac[0] = jnp.exp(running)
    fac[1] = jnp.exp(ending - running)
    fac[2] = jnp.exp(running - middle)
    fac[3] = jnp.exp(middle - running)
    fac[4] = jnp.exp(jnp.where(row < HALF, edge - running, running - edge))
    skg[...] = jnp.zeros_like(skg)
    skg[0:1, :HEADS] = skip_ref[...]
    acc[...] = jnp.zeros_like(acc)
    sk[0, 0] = jnp.zeros((8, 128), F32)

    def turned(values, k):
        return pltpu.roll(values, lax.rem(128 - CH * k, 128), 1)

    def factor(n, k):
        return expand(turned(fac[n], k))

    def row_of(values, k):
        return expand(turned(values, k)[0:1])

    def decay_row(k):
        return row_of(fac[0, TOK - 8 : TOK][7:8] + jnp.zeros((8, 128), F32), k)

    for g in range(GROUPS):
        part = b_ref[:, g * 128 : (g + 1) * 128]
        b4[g] = part
        bt[g] = part.astype(F32).T.astype(BF)

    @pl.when(s == 0)
    def _():
        er[...] = jnp.zeros_like(er)

    @pl.when(s == 3)
    def _():
        lr[...] = jnp.zeros_like(lr)

    def first(k, carried):
        get_x(k).wait()
        scaled = (factor(1, k) * xs[k].astype(F32)).astype(BF)
        x3[k] = scaled
        own[k] = dot(bt[lax.div(k, CH)], scaled).astype(BF)

        @pl.when(s == 0)
        def _():
            fwd(k).start()

        return carried

    lax.fori_loop(0, K, first, 0)
    w_wait(0, 0)
    w_start(0, 1)

    def project(q):
        weights = w[q].reshape(DIM // 2, 256)
        cp_send[q] = dot(li[1], weights)
        cp_copy(q).start()
        cp_own[q] = dot(li[0], weights)

    def projected(q):
        cp_copy(q).wait_recv()
        both = (cp_own[q] + cp_recv[q]).astype(BF)
        for n in range(2):
            g = 2 * q + n
            mine = both[:, n * 128 : (n + 1) * 128]
            cb[g] = mine
            ct[g] = mine.astype(F32).T.astype(BF)
            scores = dot_nt(mine, b4[g])
            flipped = dot_nt(b4[g], mine)
            smat[g] = jnp.where(rows_i >= cols_i, scores, 0.0).astype(BF)
            stmat[g] = jnp.where(rows_i <= cols_i, flipped, 0.0).astype(BF)

    def step(i, carried):
        f = i - s

        @pl.when((f >= 0) & (f < K) & (s > 0))
        def _():
            fwd(f).wait_recv()

            @pl.when(s < 3)
            def _():
                rounded = decay_row(f).astype(BF).astype(F32)
                own[f] = (rounded * er[f].astype(F32) + own[f].astype(F32)).astype(BF)
                fwd(f).start()

        @pl.when(i == 0)
        def _():
            w_wait(0, 1)
            w_start(0, 2)
            get_w(1).wait()
            w_start(1, 0)

        @pl.when(i == 1)
        def _():
            w_wait(0, 2)
            w_start(0, 3)
            w_wait(1, 0)
            w_start(1, 1)

        @pl.when(i == 2)
        def _():
            pltpu.make_async_copy(li.at[0], li.at[0], load_li).wait()
            remote(li.at[1], li.at[1], li_send, li_recv, sibling).wait()
            w_wait(0, 3)
            project(0)

        @pl.when(i == 3)
        def _():
            projected(0)
            w_wait(1, 1)
            w_start(1, 2)

        @pl.when(i == 4)
        def _():
            w_wait(1, 2)
            w_start(1, 3)

        @pl.when(i == 6)
        def _():
            w_wait(1, 3)
            project(1)

        @pl.when(i == 7)
        def _():
            projected(1)

        b = i - (3 - s) - OFF
        bg = lax.div(b, CH)
        active = (b >= 0) & (b < K)

        @pl.when(active & (s > 0))
        def _():
            adj[b] = dot(ct[bg], g3[b]).astype(BF)

        @pl.when(active & (s < 3))
        def _():
            bwd_wait(b)

            @pl.when(s > 0)
            def _():
                rounded = decay_row(b).astype(BF).astype(F32)
                adj[b] = (rounded * lr[b].astype(F32) + adj[b].astype(F32)).astype(BF)

        @pl.when(active & (s > 0))
        def _():
            bwd(b).start()

        @pl.when(i < K)
        def _():
            prepare(i)

        @pl.when((f >= 0) & (f < K))
        def _():
            carry(f)

        r = i - s - CH
        rg, rs = lax.div(r, CH), lax.rem(r, CH)

        @pl.when((r >= CH) & (rs == 0) & (rg <= GROUPS))
        def _():
            r_last(rg - 1, 1)

        @pl.when((r >= 0) & (rg < GROUPS))
        def _():
            @pl.when(rs == 0)
            def _():
                weight_term(rg)
                r_start(rg, 0)

            @pl.when(rs == 1)
            def _():
                r_middle(rg, 0)

            @pl.when(rs == 2)
            def _():
                r_last(rg, 0)
                r_start(rg, 2)

            @pl.when(rs == 3)
            def _():
                r_middle(rg, 1)

        @pl.when(active)
        def _():
            finish(b)

        for axis in range(4):

            @pl.when(i == K + axis)
            def _():
                if axis > 0:
                    skip_sum(axis - 1)
                for n in sk_range(axis):
                    sk_copy(axis, n).start()

        return carried

    def bwd_wait(b):
        bwd(b).wait_recv()

    def skip_sum(axis):
        total = sk[axis, 0]
        for n in sk_range(axis):
            sk_copy(axis, n).wait_recv()
            total = total + sk[axis, n]
        if axis < 3:
            sk[axis + 1, 0] = total
        else:
            dskip_ref[...] = total[0:1, :HEADS] * (1.0 / 32.0)

    def prepare(k):
        g = lax.div(k, CH)
        get_g(k).wait()
        xv = xs[k].astype(F32)
        gv = gs[k].astype(F32)
        g3[k] = (factor(0, k) * gv).astype(BF)
        gpv = (factor(2, k) * gv).astype(BF)
        xpv = (factor(3, k) * xv).astype(BF)
        cross = factor(4, k)
        x2 = (cross[:HALF] * xv[:HALF]).astype(BF)
        g2 = (cross[HALF:] * gv[HALF:]).astype(BF)
        gp[k] = gpv
        gx2[k, :HALF] = x2
        gx2[k, HALF:] = g2
        product = jnp.sum(gv * xv, axis=0, keepdims=True)
        lane8 = lane[:8]
        tally = sk[0, 0]
        for j in range(CH):
            one = jnp.sum(product[:, j * 128 : (j + 1) * 128], axis=1, keepdims=True)
            tally = jnp.where(lane8 == CH * k + j, one, tally)
        sk[0, 0] = tally
        xs[k] = xpv
        fresh = lax.rem(k, CH) == 0
        for n, (left, right) in enumerate(((gpv[:HALF], xpv[:HALF]), (g2, x2), (gpv[HALF:], xpv[HALF:]))):
            more = dot_nt(left, right)
            ds_acc[g, n] = jnp.where(fresh, 0.0, ds_acc[g, n]) + more

    def blocks_of(g):
        return (
            jnp.where(low, ds_acc[g, 0], 0.0).astype(BF),
            ds_acc[g, 1].astype(BF),
            jnp.where(low, ds_acc[g, 2], 0.0).astype(BF),
        )

    def carry(f):
        g = lax.div(f, CH)
        fresh = lax.rem(f, CH) == 0
        dc_acc[...] = jnp.where(fresh, 0.0, dc_acc[...]) + dot_nt(g3[f], er[f])

        @pl.when(lax.rem(f, CH) == CH - 1)
        def _():
            d00, d10, d11 = blocks_of(g)
            b0, b1 = b4[g, :HALF], b4[g, HALF:]
            cg[0, g, :HALF] = (dc_acc[:HALF] + dot(d00, b0)).astype(BF)
            cg[0, g, HALF:] = (dc_acc[HALF:] + dot(d10, b0) + dot(d11, b1)).astype(BF)
            cg_copy(g).start()

    def weight_term(g):
        cg_copy(g).wait_recv()
        mine = cg[0, g].astype(F32).T.astype(BF)
        other = cg[1, g].astype(F32).T.astype(BF)
        for n in range(16):
            part = slice(n * 256, (n + 1) * 256)
            term = dot(mine, li[0, :, part]) + dot(other, li[1, :, part])
            red[g, n // 4, n % 4] = term.astype(BF)

    def finish(k):
        g = lax.div(k, CH)
        sm, st = smat[g], stmat[g]
        gpv, xpv, cross = gp[k], xs[k], gx2[k]
        g3v, x3v, ev, lv = g3[k], x3[k], er[k], lr[k]
        y0 = dot(sm[:HALF, :HALF], xpv[:HALF])
        y1 = dot(sm[HALF:, HALF:], xpv[HALF:])
        yo = dot(sm[HALF:, :HALF], cross[:HALF])
        d0 = dot(st[:HALF, :HALF], gpv[:HALF])
        d1 = dot(st[HALF:, HALF:], gpv[HALF:])
        do = dot(st[:HALF, HALF:], cross[HALF:])
        yc = dot(cb[g], ev)
        zv = dot(b4[g], lv)
        cross32, gp32, xp32 = cross.astype(F32), gpv.astype(F32), xpv.astype(F32)
        zc = x3v.astype(F32) * zv
        v = g3v.astype(F32) * yc - zc
        v0 = v[:HALF] + gp32[:HALF] * y0 - xp32[:HALF] * d0 - cross32[:HALF] * do
        v1 = v[HALF:] + gp32[HALF:] * y1 - xp32[HALF:] * d1 + cross32[HALF:] * yo
        f3, f4 = factor(3, k), factor(4, k)
        direct = row_of(skg[...], k) * gs[k].astype(F32) + factor(1, k) * zv
        dx0 = direct[:HALF] + f3[:HALF] * d0 + f4[:HALF] * do
        dx1 = direct[HALF:] + f3[HALF:] * d1
        xs[k, :HALF] = dx0.astype(BF)
        xs[k, HALF:] = dx1.astype(BF)
        put_x(k).start()
        through = jnp.sum(ev.astype(F32) * lv.astype(F32), axis=0, keepdims=True)
        total = decay_row(k) * through + jnp.sum(zc, axis=0, keepdims=True)
        tally = acc[...]
        for j in range(CH):
            part = slice(j * 128, (j + 1) * 128)
            r0 = jnp.sum(v0[:, part], axis=1, keepdims=True)
            r1 = jnp.sum(v1[:, part], axis=1, keepdims=True)
            one = jnp.sum(total[:, part], axis=1, keepdims=True)
            column = jnp.concatenate([r0, r1], axis=0) + jnp.where(row == TOK - 1, one, 0.0)
            tally = jnp.where(lane == CH * k + j, column, tally)
        acc[...] = tally
        fresh = lax.rem(k, CH) == 0
        db_acc[...] = jnp.where(fresh, 0.0, db_acc[...]) + dot_nt(x3v, lv)

        @pl.when(lax.rem(k, CH) == CH - 1)
        def _():
            d00, d10, d11 = (d.astype(F32).T.astype(BF) for d in blocks_of(g))
            c0, c1 = cb[g, :HALF], cb[g, HALF:]
            there = pl.ds(pl.multiple_of(g * 128, 128), 128)
            db_ref[:HALF, there] = (db_acc[:HALF] + dot(d00, c0) + dot(d10, c1)).astype(BF)
            db_ref[HALF:, there] = (db_acc[HALF:] + dot(d11, c1)).astype(BF)

    lax.fori_loop(0, STEPS, step, 0)
    skip_sum(3)

    for n in range(1, 4):
        x_copy(n).start()
    turned_acc = acc[...].T
    dlog = jnp.dot(turned_acc, tri, precision=HIGHEST, preferred_element_type=F32)
    dlog_ref[...] = dlog[:HEADS]
    total = red[s, z, y].astype(F32)
    for n in range(1, 4):
        x_copy(n).wait_recv()
    for n in range(3):
        total = total + xr[n].astype(F32)
    fin[c, s] = total.astype(BF)
    for n in range(1, 4):
        a_copy(n).start()
    for n in range(1, 4):
        a_copy(n).wait_recv()
    p_copy().start()
    p_copy().wait_recv()
    for h in range(2):
        for g in range(GROUPS):
            dw_ref[h * 256 : (h + 1) * 256, g * 128 : (g + 1) * 128] = fin[h, g].astype(F32).T * (
                1.0 / 32.0
            )

    def drain(k, carried):
        put_x(k).wait()

        @pl.when(s < 3)
        def _():
            fwd(k).wait_send()

        @pl.when(s > 0)
        def _():
            bwd(k).wait_send()

        return carried

    lax.fori_loop(0, K, drain, 0)

    def drain_groups(g, _):
        cg_copy(g).wait_send()
        for p in range(2):
            for stage in range(4):
                for d in range(2):
                    r_copy(g, p, stage, d).wait_send()
        return _

    lax.fori_loop(0, GROUPS, drain_groups, 0)
    for q in range(2):
        cp_copy(q).wait_send()
        for p in range(2):
            for stage in range(4):
                for d in range(2):
                    w_copy(q, p, stage, d).wait_send()
    for n in range(1, 4):
        x_copy(n).wait_send()
        a_copy(n).wait_send()
    p_copy().wait_send()
    for axis in range(4):
        for n in sk_range(axis):
            sk_copy(axis, n).wait_send()


def on_device(layer_input, c_weight, head_input, b_input, log_decay, skip_gain, out_grad):
    vmem = pl.BlockSpec(memory_space=pltpu.VMEM)
    hbm = pl.BlockSpec(memory_space=pl.ANY)
    dma = pltpu.SemaphoreType.DMA

    def bf(*shape):
        return pltpu.VMEM(shape, BF)

    def f32(*shape):
        return pltpu.VMEM(shape, F32)

    chunked = (K, TOK, CW)
    states = (K, 128, CW)
    dx, db, dw, dlog, dskip = pl.pallas_call(
        kernel,
        out_shape=(
            jax.ShapeDtypeStruct((TOK, DIM), BF),
            jax.ShapeDtypeStruct((TOK, 512), BF),
            jax.ShapeDtypeStruct((512, 512), F32),
            jax.ShapeDtypeStruct((HEADS, TOK), F32),
            jax.ShapeDtypeStruct((1, HEADS), F32),
        ),
        in_specs=[hbm, hbm, hbm, vmem, vmem, vmem, hbm],
        out_specs=(hbm, vmem, vmem, vmem, vmem),
        scratch_shapes=[
            bf(*chunked),
            bf(*chunked),
            bf(*chunked),
            bf(*chunked),
            bf(*chunked),
            bf(*chunked),
            bf(2, TOK, DIM // 2),
            bf(2, 4, 4, 256, 256),
            bf(*states),
            bf(*states),
            bf(*states),
            bf(*states),
            bf(GROUPS, 4, 4, 128, 256),
            bf(GROUPS, 2, 2, 4, 32, 256),
            bf(GROUPS, 2, 2, 4, 64, 256),
            bf(GROUPS, 2, 2, 32, 256),
            bf(GROUPS, 2, 2, 64, 256),
            f32(128, TOK),
            f32(TOK, 128),
            f32(5, TOK, 128),
            f32(8, 128),
            bf(GROUPS, TOK, 128),
            bf(GROUPS, 128, TOK),
            bf(GROUPS, TOK, 128),
            bf(GROUPS, 128, TOK),
            bf(GROUPS, TOK, TOK),
            bf(GROUPS, TOK, TOK),
            f32(2, TOK, 256),
            f32(2, TOK, 256),
            f32(2, TOK, 256),
            f32(GROUPS, 3, HALF, HALF),
            f32(TOK, 128),
            f32(TOK, 128),
            bf(2, GROUPS, TOK, 128),
            f32(TOK, 128),
            bf(3, 128, 256),
            bf(2, GROUPS, 128, 256),
            f32(4, 4, 8, 128),
            dma((K,)),
            dma((K,)),
            dma,
            dma((2,)),
            dma((K,)),
            dma,
            dma,
            dma((2, 2, 4, 2)),
            dma((2, 2, 4, 2)),
            dma((K,)),
            dma((K,)),
            dma((K,)),
            dma((K,)),
            dma((2,)),
            dma((2,)),
            dma((GROUPS,)),
            dma((GROUPS,)),
            dma((GROUPS, 2, 4, 2)),
            dma((GROUPS, 2, 4, 2)),
            dma((4,)),
            dma((4,)),
            dma((4,)),
            dma((4,)),
            dma,
            dma,
            dma((4, 4)),
            dma((4, 4)),
        ],
        compiler_params=pltpu.CompilerParams(
            collective_id=0, has_side_effects=True, vmem_limit_bytes=62 * 1024 * 1024
        ),
    )(
        layer_input[0],
        c_weight,
        head_input[0],
        b_input[0],
        log_decay[0],
        skip_gain[None],
        out_grad[0],
    )
    return dx[None], db[None], dw, dlog[None], dskip[0]


def solution(mesh):
    token = P(("fsdp", "dp"), "seq", None)
    decay = P(("fsdp", "dp"), None, "seq")
    rows = P("fsdp", None)
    return jax.shard_map(
        on_device,
        mesh=mesh,
        in_specs=(token, rows, token, token, decay, P(), token),
        out_specs=(token, token, rows, decay, P()),
        check_vma=False,
    )
```

time: 423 us -> 157 us (0.37)
  waiting for transfers between devices: 162 us -> 0 us
  Pallas kernels: 0 us -> 148 us
  blocking collectives: 76.4 us -> 0 us
  matrix products: 67.9 us -> 0 us
  other arithmetic: 64.7 us -> 0 us
  local copies, waits for them, and re-layouts: 34.8 us -> 7.57 us
  between operations: 14.9 us -> 0.68 us
    pallas_call x0 -> x1, Pallas kernels: none -> 148 us  [on_device(): pl.pallas_call(kernel, out_shape=(jax.ShapeDtypeStruct((TOK, DIM), BF), j...]
    all_gather x3 -> x0, waiting for transfers between devices: 113 us -> none  [the longest x2 58.3 us: entering_2(): lax.all_gather(part.astype(kind), axis)]
    dot_general x12 -> x0, matrix products: 67.9 us -> none  [the longest x2 25.4 us: block_forward(): jnp.einsum('gkts,sgkp->tgkp', mixing, grouped, preferred_element_type=jnp...]
    psum x1 -> x0, blocking collectives: 66.9 us -> none  [on_device(): skip_total = lax.psum(skip_part, ('seq', 'fsdp', 'dp'))]
    psum x1 -> x0, waiting for transfers between devices: 48.1 us -> none  [on_device(): weight_grad = lax.psum(grad_shard, ('seq', 'dp')).astype(jnp.float32)]
    select_n x8 -> x0, other arithmetic: 46 us -> none  [turn(): return jax.tree.map(lambda a, b: jnp.where(reached, a, b), new, before)]
    unnamed x56 -> x13, local copies, waits for them, and re-layouts: 21 us -> 7.57 us
    unnamed x1 -> x0, blocking collectives: 9.47 us -> none
  transfers between devices with their start and end apart: 5 -> 0, of which waited for: 3 -> 0; matrix products, arithmetic and copies ran while one was open for 39% -> 0% of each run, Pallas kernels for 0% -> 0%
where the time goes in v1:
time: 157 us; the launch traced here: 156 us
  Pallas kernels  148 us (94%)
  local copies, waits for them, and re-layouts  7.57 us (5%)
    pallas_call x1, Pallas kernels, on_device(): pl.pallas_call(kernel, out_shape=(jax.ShapeDtypeStruct((TOK, DIM), BF), j...  148 us
    unnamed x13, local copies, waits for them, and re-layouts  7.57 us

profile of v1, /device:TPU:1, one launch (start us, length us, event | category | flops | bytes accessed | tf_op | source)
XLA Modules:
  0.0 156.4 jit_solution(3940392590612263222)
XLA Ops:
  0.6 148.1 %shard_map.110 = (bf16[256,8192]{1,0:T(8,128)(2,1)}, bf16[256,512]{1,0:T(8,128)(2,1)}, f32[512,512]{1,0:T(8,128)}, f32[64,256]{1,0:T(8,128)}, f32[1,64]{1,0:T(1,128)}) custom-call(bf16[256,8192]{1,0:T(8,128)(2,1)} %bitcast.11, bf16[512,512]{1,0:T(8,128)(2,1)} %cw_hbm.1, bf16[256,8192]{1,0:T(8,128)(2,1)} %bitcast.12, bf16[256,512]{1,0:T(8,128)(2,1)} %bitcast.15, ...), custom_call_target="tpu_custom_call" | custom-call | tf_op jit(solution)/shard_map/pallas_call | solution.py:725
  148.8 0.0 copy-start.1
  148.8 0.0 copy-start
  148.8 0.0 copy-start.2
  148.8 0.0 copy-start.3
  148.8 4.7 %copy.17 = bf16[1,256,8192]{2,1,0:T(8,128)(2,1)} copy(bf16[1,256,8192]{2,1,0:T(8,128)(2,1)} %bitcast.10) | data formatting | bytes 8388608
  153.6 0.0 copy-done.1
  153.6 0.7 copy.18
  154.3 0.0 copy-done
  154.3 1.0 copy.19
  155.2 0.0 copy-done.2
  155.2 0.6 copy.20
  155.9 0.0 copy-done.3
  155.9 0.5 copy.21
Async XLA Ops:
  148.8 4.8 %copy-start.1 = (bf16[256,512]{1,0:T(8,128)(2,1)S(1)}, bf16[256,512]{1,0:T(8,128)(2,1)}, u32[]{:S(2)}) copy-start(bf16[256,512]{1,0:T(8,128)(2,1)} %get-tuple-element.11) | copy-start | bytes 786436
  148.8 5.5 %copy-start = (f32[512,512]{1,0:T(8,128)S(1)}, f32[512,512]{1,0:T(8,128)}, u32[]{:S(2)}) copy-start(f32[512,512]{1,0:T(8,128)} %get-tuple-element.22) | copy-start | bytes 3145732
  148.8 6.4 %copy-start.2 = (f32[64,256]{1,0:T(8,128)S(1)}, f32[64,256]{1,0:T(8,128)}, u32[]{:S(2)}) copy-start(f32[64,256]{1,0:T(8,128)} %get-tuple-element.13) | copy-start | bytes 196612
  148.8 7.1 %copy-start.3 = (f32[1,64]{1,0:T(1,128)S(1)}, f32[1,64]{1,0:T(1,128)}, u32[]{:S(2)}) copy-start(f32[1,64]{1,0:T(1,128)} %get-tuple-element.14) | copy-start | bytes 772

commit v2 on v1

v2 whole, which is shorter than its diff:
```python
import jax
import jax.numpy as jnp
from jax import lax
from jax.experimental import pallas as pl
from jax.experimental.pallas import tpu as pltpu
from jax.sharding import PartitionSpec as P

HEADS = 64
GROUPS = 4
TOK = 256
HALF = 128
DIM = 8192
CH = 4
K = HEADS // CH
CW = CH * 128
AHEAD = 4
STEPS = 28
BF = jnp.bfloat16
F32 = jnp.float32
MESH = pl.DeviceIdType.MESH
HIGHEST = lax.Precision.HIGHEST
NT = (((1,), (1,)), ((), ()))


def dot(a, b):
    return jnp.dot(a, b, preferred_element_type=F32)


def dot_nt(a, b):
    return lax.dot_general(a, b, NT, preferred_element_type=F32)


def kernel(
    li_hbm,
    cw_hbm,
    x_hbm,
    b_ref,
    log_ref,
    skip_ref,
    g_hbm,
    dx_hbm,
    db_ref,
    fin,
    dlog_ref,
    dskip_ref,
    xs,
    gs,
    gb,
    xb,
    li,
    w,
    er,
    own,
    eout,
    lr,
    adj,
    red,
    t1,
    u1,
    t2,
    u2,
    ft,
    ft2,
    vals,
    b4,
    bt,
    cb,
    ct,
    ls,
    ly,
    s10,
    cp_own,
    cp_send,
    cp_recv,
    ds_acc,
    dc_acc,
    db_acc,
    cg,
    acc,
    xr,
    sk,
    load_x,
    load_g,
    load_li,
    load_w,
    store_x,
    li_send,
    li_recv,
    w_send,
    w_recv,
    f_send,
    f_recv,
    b_send,
    b_recv,
    cp_ssem,
    cp_rsem,
    cg_send,
    cg_recv,
    r_send,
    r_recv,
    x_send,
    x_recv,
    a_send,
    a_recv,
    sk_send,
    sk_recv,
):
    s = lax.axis_index("seq")
    fs = lax.axis_index("fsdp")
    c = lax.axis_index("dp")
    z, y = lax.div(fs, 4), lax.rem(fs, 4)

    def at(seq=None, zz=None, yy=None, core=None):
        seq = s if seq is None else seq
        zz = z if zz is None else zz
        yy = y if yy is None else yy
        core = c if core is None else core
        return {"seq": seq, "fsdp": zz * 4 + yy, "dp": core}

    def plus(i, n):
        return lax.rem(i + n, 4)

    def remote(src, dst, send, recv, device):
        return pltpu.make_async_remote_copy(
            src_ref=src,
            dst_ref=dst,
            send_sem=send,
            recv_sem=recv,
            device_id=device,
            device_id_type=MESH,
        )

    sibling = at(core=1 - c)

    def lanes(k):
        return pl.ds(pl.multiple_of(k * CW, CW), CW)

    def get_x(k):
        return pltpu.make_async_copy(x_hbm.at[:, lanes(k)], xs.at[k], load_x.at[k])

    def get_g(k):
        return pltpu.make_async_copy(g_hbm.at[:, lanes(k)], gs.at[k], load_g.at[k])

    def put_x(k):
        return pltpu.make_async_copy(gs.at[k], dx_hbm.at[:, lanes(k)], store_x.at[k])

    def get_w(q):
        return pltpu.make_async_copy(
            cw_hbm.at[pl.ds(pl.multiple_of(c * 256, 256), 256), pl.ds(q * 128, 128)],
            w.at[q, z, y],
            load_w.at[q],
        )

    def li_lanes(k, core):
        return pl.ds(pl.multiple_of(k * 512 + core * 256, 256), 256)

    def li_slot(slot, k):
        return li.at[slot, :, pl.ds(pl.multiple_of(k * 256, 256), 256)]

    def fwd(k):
        return remote(eout.at[k], er.at[k], f_send.at[k], f_recv.at[k], at(seq=plus(s, 1)))

    def bwd(k):
        return remote(adj.at[k], lr.at[k], b_send.at[k], b_recv.at[k], at(seq=plus(s, 3)))

    def toward(axis, d):
        if axis == 0:
            return at(zz=plus(z, 1 if d == 0 else 3))
        return at(yy=plus(y, 1 if d == 0 else 3))

    def w_copy(q, p, stage, d):
        phase, second = stage // 2, stage % 2
        axis = (1 - p) if phase == 0 else p
        me = z if axis == 0 else y
        idx = me if second == 0 else plus(me, 3 if d == 0 else 1)
        rows = pl.ds(p * 128, 128) if second == 0 else pl.ds(p * 128 + d * 64, 64)
        if phase == 0:
            ref = w.at[q, idx, y, rows] if axis == 0 else w.at[q, z, idx, rows]
        else:
            ref = w.at[q, idx, :, rows] if axis == 0 else w.at[q, :, idx, rows]
        return remote(
            ref, ref, w_send.at[q, p, stage, d], w_recv.at[q, p, stage, d], toward(axis, d)
        )

    def w_start(q, stage):
        for p in range(2):
            for d in range(2):
                w_copy(q, p, stage, d).start()

    def w_wait(q, stage):
        for p in range(2):
            for d in range(2):
                w_copy(q, p, stage, d).wait_recv()

    def cp_copy(q):
        return remote(cp_send.at[q], cp_recv.at[q], cp_ssem.at[q], cp_rsem.at[q], sibling)

    def cg_copy(g):
        return remote(cg.at[0, g], cg.at[1, g], cg_send.at[g], cg_recv.at[g], sibling)

    def r_axis(p, phase):
        return p if phase == 0 else 1 - p

    def r_ref(g, p, phase, idx, rows):
        if phase == 0:
            return red.at[g, idx, :, rows] if p == 0 else red.at[g, :, idx, rows]
        return red.at[g, z, idx, rows] if p == 0 else red.at[g, idx, y, rows]

    def r_full(p):
        return pl.ds(p * 64, 64)

    def r_half(p, h):
        return pl.ds(p * 64 + h * 32, 32)

    def r_copy(g, p, stage, d):
        phase, second = stage // 2, stage % 2
        axis = r_axis(p, phase)
        me = z if axis == 0 else y
        if second == 0:
            src = r_ref(g, p, phase, plus(me, 2), r_half(p, d))
            dst = (t1 if phase == 0 else t2).at[g, p, d]
        else:
            src = r_ref(g, p, phase, plus(me, 1 if d == 0 else 3), r_full(p))
            dst = (u1 if phase == 0 else u2).at[g, p, d]
        return remote(
            src, dst, r_send.at[g, p, stage, d], r_recv.at[g, p, stage, d], toward(axis, d)
        )

    def r_start(g, stage):
        for p in range(2):
            for d in range(2):
                r_copy(g, p, stage, d).start()

    def r_middle(g, phase):
        for p in range(2):
            me = z if r_axis(p, phase) == 0 else y
            for d in range(2):
                r_copy(g, p, 2 * phase, d).wait_recv()
                ref = r_ref(g, p, phase, plus(me, 1 if d == 0 else 3), r_half(p, d))
                got = (t1 if phase == 0 else t2)[g, p, d]
                ref[...] = (ref[...].astype(F32) + got.astype(F32)).astype(BF)
                r_copy(g, p, 2 * phase + 1, d).start()

    def r_last(g, phase):
        for p in range(2):
            me = z if r_axis(p, phase) == 0 else y
            buf = u1 if phase == 0 else u2
            for d in range(2):
                r_copy(g, p, 2 * phase + 1, d).wait_recv()
            ref = r_ref(g, p, phase, me, r_full(p))
            total = ref[...].astype(F32) + buf[g, p, 0].astype(F32) + buf[g, p, 1].astype(F32)
            ref[...] = total.astype(BF)

    def x_copy(n):
        to = plus(s, n)
        return remote(red.at[to, z, y], xr.at[n - 1], x_send.at[n], x_recv.at[n], at(seq=to))

    def a_copy(n, other):
        to = at(seq=plus(s, n), core=1 - c if other else c)
        return remote(fin.at[c, s], fin.at[c, s], a_send.at[n, other], a_recv.at[n, other], to)

    spread = [(n, other) for other in range(2) for n in range(4)][1:]

    def sk_copy(axis, n):
        if axis == 3:
            return remote(sk.at[3, 0], sk.at[3, 1], sk_send.at[3, 1], sk_recv.at[3, 1], sibling)
        to = (
            at(zz=plus(z, n))
            if axis == 0
            else (at(yy=plus(y, n)) if axis == 1 else at(seq=plus(s, n)))
        )
        return remote(sk.at[axis, 0], sk.at[axis, n], sk_send.at[axis, n], sk_recv.at[axis, n], to)

    def sk_range(axis):
        return range(1, 2) if axis == 3 else range(1, 4)

    for q in range(4):
        get_w(q).start()

    def load(k, carried):
        get_x(k).start()
        return carried

    lax.fori_loop(0, K, load, 0)

    barrier = pltpu.get_barrier_semaphore()
    peers = [sibling]
    for n in range(1, 4):
        peers += [at(seq=plus(s, n)), at(zz=plus(z, n)), at(yy=plus(y, n))]
        peers += [at(seq=plus(s, n), core=1 - c)]
    for peer in peers:
        pl.semaphore_signal(barrier, inc=1, device_id=peer, device_id_type=MESH)

    def load_more(k, carried):
        get_g(k).start()
        return carried

    lax.fori_loop(0, K, load_more, 0)

    rows_i = lax.broadcasted_iota(jnp.int32, (TOK, TOK), 0)
    cols_i = lax.broadcasted_iota(jnp.int32, (TOK, TOK), 1)
    tri = jnp.where(cols_i <= rows_i, 1.0, 0.0).astype(F32)
    low = rows_i[:HALF, :HALF] >= cols_i[:HALF, :HALF]
    high = rows_i[:HALF, :HALF] <= cols_i[:HALF, :HALF]
    lane = lax.broadcasted_iota(jnp.int32, (TOK, 128), 1)
    row = lax.broadcasted_iota(jnp.int32, (TOK, 128), 0)
    row128 = lax.broadcasted_iota(jnp.int32, (HALF, 1), 0)
    picks = jnp.where(
        lax.rem(lax.broadcasted_iota(jnp.int32, (2 * CH, CW), 0), CH)
        == lax.div(lax.broadcasted_iota(jnp.int32, (2 * CH, CW), 1), 128),
        1.0,
        0.0,
    ).astype(BF)

    running = lax.dot_general(log_ref[...], tri, NT, precision=HIGHEST, preferred_element_type=F32)
    ending = running[:, TOK - 1 : TOK]
    mid0 = running[:, HALF // 2 - 1 : HALF // 2]
    mid1 = running[:, HALF + HALF // 2 - 1 : HALF + HALF // 2]
    for n, value in enumerate((ending, ending - mid0, ending - mid1, mid0, mid1)):
        vals[n] = jnp.broadcast_to(jnp.exp(value), (HEADS, 128))
    gain = jnp.concatenate([skip_ref[...]] * 2, axis=1)
    gains = jnp.where(lane[:HEADS] == row[:HEADS], gain, 0.0)
    vals[5] = jnp.broadcast_to(jnp.sum(gains, axis=1, keepdims=True), (HEADS, 128))
    middle = jnp.where(cols_i[:HEADS] < HALF, mid0, mid1)

    def split(values):
        coarse = values.astype(BF).astype(F32)
        return coarse, (values - coarse).astype(BF).astype(F32)

    for n, values in enumerate((running - middle, middle - running)):
        for half, part in enumerate(split(jnp.exp(values))):
            for k in range(K):
                ft[n, k, half * CH : (half + 1) * CH] = part[k * CH : (k + 1) * CH]
    for half, part in enumerate(split(jnp.exp(running[:, HALF:] - mid0))):
        for k in range(K):
            ft2[k, half * CH : (half + 1) * CH] = part[k * CH : (k + 1) * CH]
    acc[...] = jnp.zeros_like(acc)
    sk[0, 0] = jnp.zeros((8, 128), F32)

    def factor(n, k):
        return dot(ft[n, k].T.astype(BF), picks)

    def row_of(n, k):
        return jnp.concatenate([vals[n, pl.ds(CH * k + j, 1), :] for j in range(CH)], axis=1)

    for g in range(GROUPS):
        part = b_ref[:, g * 128 : (g + 1) * 128]
        b4[g] = part
        bt[g] = part.astype(F32).T.astype(BF)
        ls[g, :HALF, 256:] = part[:HALF]
        ls[g, HALF:, 128:256] = part[HALF:]

    @pl.when(s == 0)
    def _():
        er[...] = jnp.zeros_like(er)

    @pl.when(s == 3)
    def _():
        lr[...] = jnp.zeros_like(lr)
        own[...] = jnp.zeros_like(own)

    def first(k):
        g = lax.div(k, CH)
        get_x(k).wait()
        scaled = (factor(1, k) * xs[k].astype(F32)).astype(BF)
        xb[k, :128] = scaled[:HALF]
        xb[k, 256:384] = scaled[HALF:]

        @pl.when(s < 3)
        def _():
            state = row_of(1, k) * dot(bt[g, :, :HALF], scaled[:HALF])
            state = (state + row_of(2, k) * dot(bt[g, :, HALF:], scaled[HALF:])).astype(BF)
            own[k] = state

            @pl.when(s == 0)
            def _():
                eout[k] = state
                fwd(k).start()

    pl.semaphore_wait(barrier, len(peers))
    for q in range(4):
        get_w(q).wait()
        w_start(q, 0)

    def load_part(k, carried):
        pltpu.make_async_copy(li_hbm.at[:, li_lanes(k, c)], li_slot(0, k), load_li).start()
        remote(li_hbm.at[:, li_lanes(k, 1 - c)], li_slot(1, k), li_send, li_recv, sibling).start()
        return carried

    lax.fori_loop(0, 16, load_part, 0)

    def first_of(k, carried):
        first(k)
        return carried

    lax.fori_loop(0, AHEAD, first_of, 0)
    for q in range(4):
        w_wait(q, 0)
        w_start(q, 1)
    w_wait(0, 1)
    w_start(0, 2)

    pairs = lax.div(s * (s - 1), 2)
    triples = lax.div(s * (s - 1) * (s - 2), 6)
    slot_a = 1 + 2 * s - 3 * pairs + 2 * triples
    slot_b = 3 + 2 * s - 3 * pairs + triples
    slot_c = 5 + s - pairs - 3 * triples
    slot_d = slot_c + 2
    slot_e = slot_c + 4
    trail = 9 - s - pairs - triples

    def project(q):
        weights = w[q].reshape(DIM // 2, 128)
        cp_send[q] = dot(li[1], weights)
        cp_copy(q).start()
        cp_own[q] = dot(li[0], weights)

    def projected(g):
        cp_copy(g).wait_recv()
        mine = (cp_own[g] + cp_recv[g]).astype(BF)
        cb[g] = mine
        ct[g] = mine.astype(F32).T.astype(BF)
        scores = dot_nt(mine, b4[g])
        flipped = dot_nt(b4[g], mine)
        ly[g, :HALF, :128] = jnp.where(low, scores[:HALF, :HALF], 0.0).astype(BF)
        ly[g, HALF:, :128] = jnp.where(low, scores[HALF:, HALF:], 0.0).astype(BF)
        ly[g, :, 128:] = mine
        s10[g] = scores[HALF:, :HALF].astype(BF)
        ls[g, :HALF, :128] = jnp.where(high, flipped[:HALF, :HALF], 0.0).astype(BF)
        ls[g, :HALF, 128:256] = flipped[:HALF, HALF:].astype(BF)
        ls[g, HALF:, :128] = jnp.where(high, flipped[HALF:, HALF:], 0.0).astype(BF)

    def step(i, carried):
        f = i - s

        @pl.when((f >= 0) & (f < K) & (s > 0))
        def _():
            fwd(f).wait_recv()

            @pl.when(s < 3)
            def _():
                rounded = row_of(0, f).astype(BF).astype(F32)
                eout[f] = (rounded * er[f].astype(F32) + own[f].astype(F32)).astype(BF)
                fwd(f).start()

        @pl.when(i + AHEAD < K)
        def _():
            first(i + AHEAD)

        for g, slot in enumerate((slot_b, slot_c, slot_d, slot_e)):

            @pl.when(i == slot + 1)
            def _():
                projected(g)

        b = i - trail

        @pl.when((b >= 0) & (b < K))
        def _():
            bg = lax.div(b, CH)

            @pl.when(s > 0)
            def _():
                term = row_of(3, b) * dot(ct[bg, :, :HALF], gb[b, :128])
                term = term + row_of(4, b) * dot(ct[bg, :, HALF:], gb[b, 384:512])
                adj[b] = term.astype(BF)

            @pl.when(s < 3)
            def _():
                bwd(b).wait_recv()

                @pl.when(s > 0)
                def _():
                    rounded = row_of(0, b).astype(BF).astype(F32)
                    adj[b] = (rounded * lr[b].astype(F32) + adj[b].astype(F32)).astype(BF)

            @pl.when(s > 0)
            def _():
                bwd(b).start()

        @pl.when(i == slot_a)
        def _():
            w_wait(0, 2)
            w_start(0, 3)
            w_wait(1, 1)
            w_start(1, 2)

        @pl.when(i == slot_b)
        def _():
            pltpu.make_async_copy(li.at[0], li.at[0], load_li).wait()
            remote(li.at[1], li.at[1], li_send, li_recv, sibling).wait()
            w_wait(0, 3)
            project(0)
            w_wait(1, 2)
            w_start(1, 3)
            w_wait(2, 1)
            w_start(2, 2)

        @pl.when(i == slot_c)
        def _():
            w_wait(1, 3)
            project(1)
            w_wait(2, 2)
            w_start(2, 3)
            w_wait(3, 1)
            w_start(3, 2)

        @pl.when(i == slot_d)
        def _():
            w_wait(2, 3)
            project(2)
            w_wait(3, 2)
            w_start(3, 3)

        @pl.when(i == slot_e)
        def _():
            w_wait(3, 3)
            project(3)

        @pl.when(i < K)
        def _():
            prepare(i)

        @pl.when((f >= 0) & (f < K))
        def _():
            carry(f)

        @pl.when((b >= 1) & (b <= K))
        def _():
            finish(b - 1)

        for stage in range(5):
            r = f - CH - 2 * stage

            @pl.when((r >= 0) & (r < GROUPS * CH) & (lax.rem(r, CH) == 0))
            def _():
                g = lax.div(r, CH)
                if stage == 0:
                    weight_term(g)
                    r_start(g, 0)
                elif stage == 1:
                    r_middle(g, 0)
                elif stage == 2:
                    r_last(g, 0)
                    r_start(g, 2)
                elif stage == 3:
                    r_middle(g, 1)
                else:
                    r_last(g, 1)

        for axis in range(5):

            @pl.when(i == K + 1 + 2 * axis)
            def _():
                if axis > 0:
                    skip_sum(axis - 1)
                if axis < 4:
                    for n in sk_range(axis):
                        sk_copy(axis, n).start()

        return carried

    def skip_sum(axis):
        total = sk[axis, 0]
        for n in sk_range(axis):
            sk_copy(axis, n).wait_recv()
            total = total + sk[axis, n]
        if axis < 3:
            sk[axis + 1, 0] = total
        else:
            dskip_ref[...] = total[0:1, :HEADS] * (1.0 / 32.0)

    def prepare(k):
        g = lax.div(k, CH)
        get_g(k).wait()
        xv = xs[k].astype(F32)
        gv = gs[k].astype(F32)
        scaled = (factor(0, k) * gv).astype(BF)
        gb[k, :128] = scaled[:HALF]
        gb[k, 384:512] = scaled[HALF:]
        gb[k, 128:256] = (dot(ft2[k].T.astype(BF), picks) * gv[HALF:]).astype(BF)
        product = jnp.sum(gv * xv, axis=0, keepdims=True)
        lane8 = lane[:8]
        tally = sk[0, 0]
        for j in range(CH):
            one = jnp.sum(product[:, j * 128 : (j + 1) * 128], axis=1, keepdims=True)
            tally = jnp.where(lane8 == CH * k + j, one, tally)
        sk[0, 0] = tally
        fresh = lax.rem(k, CH) == 0
        more = dot_nt(gb[k, :256], xb[k, :128])
        ds_acc[g, :256] = jnp.where(fresh, 0.0, ds_acc[g, :256]) + more
        more = dot_nt(scaled[HALF:], xb[k, 256:384])
        ds_acc[g, 256:] = jnp.where(fresh, 0.0, ds_acc[g, 256:]) + more

    def blocks_of(g):
        return (
            jnp.where(low, ds_acc[g, :128], 0.0),
            ds_acc[g, 128:256],
            jnp.where(low, ds_acc[g, 256:], 0.0),
        )

    def carry(f):
        g = lax.div(f, CH)
        fresh = lax.rem(f, CH) == 0
        ev = er[f].astype(F32)
        for n in range(2):
            scaled = (row_of(3 + n, f) * ev).astype(BF)
            xb[f, 128 + 256 * n : 256 + 256 * n] = scaled
            half = slice(n * HALF, (n + 1) * HALF)
            more = dot_nt(gb[f, 384 * n : 384 * n + 128], scaled)
            dc_acc[half] = jnp.where(fresh, 0.0, dc_acc[half]) + more

        @pl.when(lax.rem(f, CH) == CH - 1)
        def _():
            d00, d10, d11 = (d.astype(BF) for d in blocks_of(g))
            b0, b1 = b4[g, :HALF], b4[g, HALF:]
            cg[0, g, :HALF] = (dc_acc[:HALF] + dot(d00, b0)).astype(BF)
            cg[0, g, HALF:] = (dc_acc[HALF:] + dot(d10, b0) + dot(d11, b1)).astype(BF)
            cg_copy(g).start()

    def weight_term(g):
        cg_copy(g).wait_recv()
        mine = cg[0, g].astype(F32).T.astype(BF)
        other = cg[1, g].astype(F32).T.astype(BF)
        for n in range(16):
            part = slice(n * 256, (n + 1) * 256)
            term = dot(mine, li[0, :, part]) + dot(other, li[1, :, part])
            red[g, n // 4, n % 4] = term.astype(BF)

    def finish(k):
        g = lax.div(k, CH)
        lv = lr[k].astype(F32)
        fresh = lax.rem(k, CH) == 0
        for n, there in enumerate((256, 512)):
            scaled = (row_of(1 + n, k) * lv).astype(BF)
            gb[k, there : there + 128] = scaled
            half = slice(n * HALF, (n + 1) * HALF)
            more = dot_nt(xb[k, 256 * n : 256 * n + 128], scaled)
            db_acc[half] = jnp.where(fresh, 0.0, db_acc[half]) + more
        back = factor(1, k)
        gain = row_of(5, k)
        through = row_of(0, k) * jnp.sum(er[k].astype(F32) * lv, axis=0, keepdims=True)
        through = through + jnp.sum(own[k].astype(F32) * lv, axis=0, keepdims=True)
        heads = jnp.where(
            lax.broadcasted_iota(jnp.int32, (CW, 128), 1)
            == CH * k + lax.div(lax.broadcasted_iota(jnp.int32, (CW, 128), 0), 128),
            1.0,
            0.0,
        ).astype(BF)
        for n in range(2):
            half = slice(n * HALF, (n + 1) * HALF)
            if n == 0:
                dxs = dot(ls[g, :HALF], gb[k, :384])
                ys = dot(ly[g, :HALF], xb[k, :256])
                v = gb[k, :128].astype(F32) * ys - xb[k, :128].astype(F32) * dxs
            else:
                dxs = dot(ls[g, HALF:, :256], gb[k, 384:640])
                ys = dot(ly[g, HALF:], xb[k, 256:512])
                v = gb[k, 384:512].astype(F32) * ys - xb[k, 256:384].astype(F32) * dxs
                v = v + gb[k, 128:256].astype(F32) * dot(s10[g], xb[k, :128])
                v = v + jnp.where(row128 == HALF - 1, through, 0.0)
            gs[k, half] = (gain * gs[k, half].astype(F32) + back[half] * dxs).astype(BF)
            coarse = v.astype(BF)
            rest = (v - coarse.astype(F32)).astype(BF)
            acc[half] += dot(coarse, heads) + dot(rest, heads)
        put_x(k).start()
        @pl.when(lax.rem(k, CH) == CH - 1)
        def _():
            d00, d10, d11 = (d.T.astype(BF) for d in blocks_of(g))
            c0, c1 = cb[g, :HALF], cb[g, HALF:]
            there = pl.ds(pl.multiple_of(g * 128, 128), 128)
            db_ref[:HALF, there] = (db_acc[:HALF] + dot(d00, c0) + dot(d10, c1)).astype(BF)
            db_ref[HALF:, there] = (db_acc[HALF:] + dot(d11, c1)).astype(BF)

    lax.fori_loop(0, STEPS, step, 0)
    for n in range(1, 4):
        x_copy(n).start()
    turned_acc = acc[...].T
    dlog = jnp.dot(turned_acc, tri, precision=HIGHEST, preferred_element_type=F32)
    dlog_ref[...] = dlog[:HEADS]
    total = red[s, z, y].astype(F32)
    for n in range(1, 4):
        x_copy(n).wait_recv()
    for n in range(3):
        total = total + xr[n].astype(F32)
    fin[c, s] = total.astype(BF)
    for n, other in spread:
        a_copy(n, other).start()
    for n, other in spread:
        a_copy(n, other).wait_recv()

    def drain(k, carried):
        put_x(k).wait()

        @pl.when(s < 3)
        def _():
            fwd(k).wait_send()

        @pl.when(s > 0)
        def _():
            bwd(k).wait_send()

        return carried

    lax.fori_loop(0, K, drain, 0)

    def drain_groups(g, _):
        cg_copy(g).wait_send()
        for p in range(2):
            for stage in range(4):
                for d in range(2):
                    r_copy(g, p, stage, d).wait_send()
        return _

    lax.fori_loop(0, GROUPS, drain_groups, 0)
    for q in range(4):
        cp_copy(q).wait_send()
        for p in range(2):
            for stage in range(4):
                for d in range(2):
                    w_copy(q, p, stage, d).wait_send()
    for n in range(1, 4):
        x_copy(n).wait_send()
    for n, other in spread:
        a_copy(n, other).wait_send()
    for axis in range(4):
        for n in sk_range(axis):
            sk_copy(axis, n).wait_send()


def publish(
    dx_in, fin_in, db_in, dlog_in, dskip_in, dx_out, dw_out, db_out, dlog_out, dskip_out,
    dx_held, fin, db_held, dlog_held, dskip_held, came, left,
):
    rows = [pl.ds(n * 32, 32) for n in range(8)]
    moves = [(fin_in, fin, None)]
    moves += [(dx_in.at[r], dx_held.at[r], dx_out.at[r]) for r in rows]
    moves += [(db_in, db_held, db_out), (dlog_in, dlog_held, dlog_out)]
    moves += [(dskip_in, dskip_held, dskip_out)]
    loads = [pltpu.make_async_copy(m[0], m[1], came.at[n]) for n, m in enumerate(moves)]
    stores = [pltpu.make_async_copy(m[1], m[2], left.at[n]) for n, m in enumerate(moves) if n > 0]
    for copy in loads:
        copy.start()
    loads[0].wait()
    for load, store in zip(loads[1:], stores):
        load.wait()
        store.start()
    for h in range(2):
        for g in range(GROUPS):
            dw_out[h * 256 : (h + 1) * 256, g * 128 : (g + 1) * 128] = fin[h, g].astype(F32).T * (
                1.0 / 32.0
            )
    for copy in stores:
        copy.wait()


def on_device(layer_input, c_weight, head_input, b_input, log_decay, skip_gain, out_grad):
    vmem = pl.BlockSpec(memory_space=pltpu.VMEM)
    hbm = pl.BlockSpec(memory_space=pl.ANY)
    dma = pltpu.SemaphoreType.DMA

    def bf(*shape):
        return pltpu.VMEM(shape, BF)

    def f32(*shape):
        return pltpu.VMEM(shape, F32)

    chunked = (K, TOK, CW)
    states = (K, 128, CW)
    dx, db, fin, dlog, dskip = pl.pallas_call(
        kernel,
        out_shape=(
            jax.ShapeDtypeStruct((TOK, DIM), BF),
            jax.ShapeDtypeStruct((TOK, 512), BF),
            jax.ShapeDtypeStruct((2, GROUPS, 128, 256), BF),
            jax.ShapeDtypeStruct((HEADS, TOK), F32),
            jax.ShapeDtypeStruct((1, HEADS), F32),
        ),
        in_specs=[hbm, hbm, hbm, vmem, vmem, vmem, hbm],
        out_specs=(hbm, vmem, vmem, vmem, vmem),
        scratch_shapes=[
            bf(*chunked),
            bf(*chunked),
            bf(K, 640, CW),
            bf(K, 512, CW),
            bf(2, TOK, DIM // 2),
            bf(4, 4, 4, 256, 128),
            bf(*states),
            bf(*states),
            bf(*states),
            bf(*states),
            bf(*states),
            bf(GROUPS, 4, 4, 128, 256),
            bf(GROUPS, 2, 2, 4, 32, 256),
            bf(GROUPS, 2, 2, 4, 64, 256),
            bf(GROUPS, 2, 2, 32, 256),
            bf(GROUPS, 2, 2, 64, 256),
            f32(2, K, 2 * CH, TOK),
            f32(K, 2 * CH, HALF),
            f32(6, HEADS, 128),
            bf(GROUPS, TOK, 128),
            bf(GROUPS, 128, TOK),
            bf(GROUPS, TOK, 128),
            bf(GROUPS, 128, TOK),
            bf(GROUPS, TOK, 384),
            bf(GROUPS, TOK, 256),
            bf(GROUPS, HALF, HALF),
            f32(GROUPS, TOK, 128),
            f32(GROUPS, TOK, 128),
            f32(GROUPS, TOK, 128),
            f32(GROUPS, 384, HALF),
            f32(TOK, 128),
            f32(TOK, 128),
            bf(2, GROUPS, TOK, 128),
            f32(TOK, 128),
            bf(3, 128, 256),
            f32(4, 4, 8, 128),
            dma((K,)),
            dma((K,)),
            dma,
            dma((4,)),
            dma((K,)),
            dma,
            dma,
            dma((4, 2, 4, 2)),
            dma((4, 2, 4, 2)),
            dma((K,)),
            dma((K,)),
            dma((K,)),
            dma((K,)),
            dma((4,)),
            dma((4,)),
            dma((GROUPS,)),
            dma((GROUPS,)),
            dma((GROUPS, 2, 4, 2)),
            dma((GROUPS, 2, 4, 2)),
            dma((4,)),
            dma((4,)),
            dma((4, 2)),
            dma((4, 2)),
            dma((4, 4)),
            dma((4, 4)),
        ],
        compiler_params=pltpu.CompilerParams(
            collective_id=0, has_side_effects=True, vmem_limit_bytes=62 * 1024 * 1024
        ),
    )(
        layer_input[0],
        c_weight,
        head_input[0],
        b_input[0],
        log_decay[0],
        skip_gain[None],
        out_grad[0],
    )
    dx, dw, db, dlog, dskip = pl.pallas_call(
        publish,
        out_shape=(
            jax.ShapeDtypeStruct((TOK, DIM), BF),
            jax.ShapeDtypeStruct((512, 512), F32),
            jax.ShapeDtypeStruct((TOK, 512), BF),
            jax.ShapeDtypeStruct((HEADS, TOK), F32),
            jax.ShapeDtypeStruct((1, HEADS), F32),
        ),
        in_specs=[hbm] * 5,
        out_specs=(hbm, vmem, hbm, hbm, hbm),
        scratch_shapes=[
            bf(TOK, DIM),
            bf(2, GROUPS, 128, 256),
            bf(TOK, 512),
            f32(HEADS, TOK),
            f32(1, HEADS),
            dma((12,)),
            dma((12,)),
        ],
        compiler_params=pltpu.CompilerParams(vmem_limit_bytes=62 * 1024 * 1024),
    )(dx, fin, db, dlog, dskip)
    return dx[None], db[None], dw, dlog[None], dskip[0]


def solution(mesh):
    token = P(("fsdp", "dp"), "seq", None)
    decay = P(("fsdp", "dp"), None, "seq")
    rows = P("fsdp", None)
    return jax.shard_map(
        on_device,
        mesh=mesh,
        in_specs=(token, rows, token, token, decay, P(), token),
        out_specs=(token, token, rows, decay, P()),
        check_vma=False,
    )
```

time: 157 us -> 119 us (0.76)
  Pallas kernels: 148 us -> 118 us
  local copies, waits for them, and re-layouts: 7.57 us -> 0 us
    pallas_call x1, Pallas kernels: 148 us -> 113 us  [on_device(): pl.pallas_call(kernel, out_shape=(jax.ShapeDtypeStruct((TOK, DIM), BF), j...]
    unnamed x13 -> x0, local copies, waits for them, and re-layouts: 7.57 us -> none
    pallas_call x0 -> x1, Pallas kernels: none -> 4.97 us  [on_device(): pl.pallas_call(publish, out_shape=(jax.ShapeDtypeStruct((TOK, DIM), BF),...]
where the time goes in v2:
time: 119 us; the launch traced here: 118 us
  Pallas kernels  118 us (99%)
    pallas_call x1, Pallas kernels, on_device(): pl.pallas_call(kernel, out_shape=(jax.ShapeDtypeStruct((TOK, DIM), BF), j...  113 us
    pallas_call x1, Pallas kernels, on_device(): pl.pallas_call(publish, out_shape=(jax.ShapeDtypeStruct((TOK, DIM), BF),...  4.97 us

profile of v2, /device:TPU:1, one launch (start us, length us, event | category | flops | bytes accessed | tf_op | source)
XLA Modules:
  0.0 118.5 jit_solution(14660104421111558819)
XLA Ops:
  0.6 112.9 %shard_map.110 = (bf16[256,8192]{1,0:T(8,128)(2,1)}, bf16[256,512]{1,0:T(8,128)(2,1)}, bf16[2,4,128,256]{3,2,1,0:T(8,128)(2,1)}, f32[64,256]{1,0:T(8,128)}, f32[1,64]{1,0:T(1,128)}) custom-call(bf16[256,8192]{1,0:T(8,128)(2,1)} %bitcast.10, bf16[512,512]{1,0:T(8,128)(2,1)} %cw_hbm.1, bf16[256,8192]{1,0:T(8,128)(2,1)} %bitcast.11, bf16[256,512]{1,0:T(8,128)(2,1)} %bitcast.13, ...), custom_call_target="tpu_custom_call" | custom-call | tf_op jit(solution)/shard_map/pallas_call | solution.py:770
  113.5 5.0 %shard_map.111 = (bf16[256,8192]{1,0:T(8,128)(2,1)}, f32[512,512]{1,0:T(8,128)}, bf16[256,512]{1,0:T(8,128)(2,1)}, f32[64,256]{1,0:T(8,128)}, f32[1,64]{1,0:T(1,128)}) custom-call(bf16[256,8192]{1,0:T(8,128)(2,1)} %get-tuple-element.15.dx_in, bf16[2,4,128,256]{3,2,1,0:T(8,128)(2,1)} %get-tuple-element.16.fin_in, bf16[256,512]{1,0:T(8,128)(2,1)} %get-tuple-element.17.db_in, ...), custom_call_target="tpu_custom_call" | custom-call | tf_op jit(solution)/shard_map/pallas_call | solution.py:856

commit v3 on v2

--- a/solution.py
+++ b/solution.py
@@ -14,7 +14,7 @@
 K = HEADS // CH
 CW = CH * 128
 AHEAD = 4
-STEPS = 28
+STEPS = 26
 BF = jnp.bfloat16
 F32 = jnp.float32
 MESH = pl.DeviceIdType.MESH
@@ -142,7 +142,7 @@
         return pltpu.make_async_copy(g_hbm.at[:, lanes(k)], gs.at[k], load_g.at[k])
 
     def put_x(k):
-        return pltpu.make_async_copy(gs.at[k], dx_hbm.at[:, lanes(k)], store_x.at[k])
+        return pltpu.make_async_copy(gs.at[k], dx_hbm.at[:, lanes(k)], store_x)
 
     def get_w(q):
         return pltpu.make_async_copy(
@@ -158,10 +158,10 @@
         return li.at[slot, :, pl.ds(pl.multiple_of(k * 256, 256), 256)]
 
     def fwd(k):
-        return remote(eout.at[k], er.at[k], f_send.at[k], f_recv.at[k], at(seq=plus(s, 1)))
+        return remote(eout.at[k], er.at[k], f_send, f_recv.at[k], at(seq=plus(s, 1)))
 
     def bwd(k):
-        return remote(adj.at[k], lr.at[k], b_send.at[k], b_recv.at[k], at(seq=plus(s, 3)))
+        return remote(adj.at[k], lr.at[k], b_send, b_recv.at[k], at(seq=plus(s, 3)))
 
     def toward(axis, d):
         if axis == 0:
@@ -175,12 +175,10 @@
         idx = me if second == 0 else plus(me, 3 if d == 0 else 1)
         rows = pl.ds(p * 128, 128) if second == 0 else pl.ds(p * 128 + d * 64, 64)
         if phase == 0:
-            ref = w.at[q, idx, y, rows] if axis == 0 else w.at[q, z, idx, rows]
+            ref = w.at[:, idx, y, rows] if axis == 0 else w.at[:, z, idx, rows]
         else:
             ref = w.at[q, idx, :, rows] if axis == 0 else w.at[q, :, idx, rows]
-        return remote(
-            ref, ref, w_send.at[q, p, stage, d], w_recv.at[q, p, stage, d], toward(axis, d)
-        )
+        return remote(ref, ref, w_send.at[stage], w_recv.at[q, stage], toward(axis, d))
 
     def w_start(q, stage):
         for p in range(2):
@@ -188,15 +186,18 @@
                 w_copy(q, p, stage, d).start()
 
     def w_wait(q, stage):
-        for p in range(2):
-            for d in range(2):
-                w_copy(q, p, stage, d).wait_recv()
+        ref = w.at[q, 0:2] if stage % 2 == 0 else w.at[q, 0]
+        remote(ref, ref, w_send.at[stage], w_recv.at[q, stage], sibling).wait_recv()
+
+    def w_sent(stage):
+        ref = (w.at[0, 0:2], w.at[0, 0], w.at[0:2], w.at[0])[stage]
+        remote(ref, ref, w_send.at[stage], w_recv.at[0, stage], sibling).wait_send()
 
     def cp_copy(q):
-        return remote(cp_send.at[q], cp_recv.at[q], cp_ssem.at[q], cp_rsem.at[q], sibling)
+        return remote(cp_send.at[q], cp_recv.at[q], cp_ssem, cp_rsem.at[q], sibling)
 
     def cg_copy(g):
-        return remote(cg.at[0, g], cg.at[1, g], cg_send.at[g], cg_recv.at[g], sibling)
+        return remote(cg.at[0, g], cg.at[1, g], cg_send, cg_recv.at[g], sibling)
 
     def r_axis(p, phase):
         return p if phase == 0 else 1 - p
@@ -222,9 +223,15 @@
         else:
             src = r_ref(g, p, phase, plus(me, 1 if d == 0 else 3), r_full(p))
             dst = (u1 if phase == 0 else u2).at[g, p, d]
-        return remote(
-            src, dst, r_send.at[g, p, stage, d], r_recv.at[g, p, stage, d], toward(axis, d)
-        )
+        return remote(src, dst, r_send.at[stage], r_recv.at[g, stage], toward(axis, d))
+
+    def r_wait(g, stage):
+        ref = (t1, u1, t2, u2)[stage].at[g]
+        remote(ref, ref, r_send.at[stage], r_recv.at[g, stage], sibling).wait_recv()
+
+    def r_sent(stage):
+        ref = (t1, u1, t2, u2)[stage]
+        remote(ref, ref, r_send.at[stage], r_recv.at[0, stage], sibling).wait_send()
 
     def r_start(g, stage):
         for p in range(2):
@@ -232,44 +239,54 @@
                 r_copy(g, p, stage, d).start()
 
     def r_middle(g, phase):
+        r_wait(g, 2 * phase)
         for p in range(2):
             me = z if r_axis(p, phase) == 0 else y
             for d in range(2):
-                r_copy(g, p, 2 * phase, d).wait_recv()
                 ref = r_ref(g, p, phase, plus(me, 1 if d == 0 else 3), r_half(p, d))
                 got = (t1 if phase == 0 else t2)[g, p, d]
                 ref[...] = (ref[...].astype(F32) + got.astype(F32)).astype(BF)
                 r_copy(g, p, 2 * phase + 1, d).start()
 
     def r_last(g, phase):
+        r_wait(g, 2 * phase + 1)
         for p in range(2):
             me = z if r_axis(p, phase) == 0 else y
             buf = u1 if phase == 0 else u2
-            for d in range(2):
-                r_copy(g, p, 2 * phase + 1, d).wait_recv()
             ref = r_ref(g, p, phase, me, r_full(p))
             total = ref[...].astype(F32) + buf[g, p, 0].astype(F32) + buf[g, p, 1].astype(F32)
             ref[...] = total.astype(BF)
 
     def x_copy(n):
         to = plus(s, n)
-        return remote(red.at[to, z, y], xr.at[n - 1], x_send.at[n], x_recv.at[n], at(seq=to))
+        return remote(red.at[to, z, y], xr.at[n - 1], x_send, x_recv, at(seq=to))
 
     def a_copy(n, other):
         to = at(seq=plus(s, n), core=1 - c if other else c)
-        return remote(fin.at[c, s], fin.at[c, s], a_send.at[n, other], a_recv.at[n, other], to)
+        return remote(fin.at[c, s], fin.at[c, s], a_send.at[other], a_recv.at[other], to)
 
     spread = [(n, other) for other in range(2) for n in range(4)][1:]
 
     def sk_copy(axis, n):
         if axis == 3:
-            return remote(sk.at[3, 0], sk.at[3, 1], sk_send.at[3, 1], sk_recv.at[3, 1], sibling)
+            return remote(sk.at[3, 0], sk.at[3, 1], sk_send.at[3], sk_recv.at[3], sibling)
         to = (
             at(zz=plus(z, n))
             if axis == 0
             else (at(yy=plus(y, n)) if axis == 1 else at(seq=plus(s, n)))
         )
-        return remote(sk.at[axis, 0], sk.at[axis, n], sk_send.at[axis, n], sk_recv.at[axis, n], to)
+        return remote(sk.at[axis, 0], sk.at[axis, n], sk_send.at[axis], sk_recv.at[axis], to)
+
+    def sk_all(axis):
+        ref = sk.at[3, 1] if axis == 3 else sk.at[axis, 1:4]
+        return remote(ref, ref, sk_send.at[axis], sk_recv.at[axis], sibling)
+
+    def a_all(other):
+        ref = fin.at[0] if other else fin.at[0, 0:3]
+        return remote(ref, ref, a_send.at[other], a_recv.at[other], sibling)
+
+    def x_all():
+        return remote(xr, xr, x_send, x_recv, sibling)
 
     def sk_range(axis):
         return range(1, 2) if axis == 3 else range(1, 4)
@@ -380,7 +397,7 @@
     pl.semaphore_wait(barrier, len(peers))
     for q in range(4):
         get_w(q).wait()
-        w_start(q, 0)
+    w_start(0, 0)
 
     def load_part(k, carried):
         pltpu.make_async_copy(li_hbm.at[:, li_lanes(k, c)], li_slot(0, k), load_li).start()
@@ -394,9 +411,8 @@
         return carried
 
     lax.fori_loop(0, AHEAD, first_of, 0)
-    for q in range(4):
-        w_wait(q, 0)
-        w_start(q, 1)
+    w_wait(0, 0)
+    w_start(0, 1)
     w_wait(0, 1)
     w_start(0, 2)
 
@@ -482,7 +498,6 @@
         def _():
             w_wait(0, 2)
             w_start(0, 3)
-            w_wait(1, 1)
             w_start(1, 2)
 
         @pl.when(i == slot_b)
@@ -493,7 +508,6 @@
             project(0)
             w_wait(1, 2)
             w_start(1, 3)
-            w_wait(2, 1)
             w_start(2, 2)
 
         @pl.when(i == slot_c)
@@ -502,7 +516,6 @@
             project(1)
             w_wait(2, 2)
             w_start(2, 3)
-            w_wait(3, 1)
             w_start(3, 2)
 
         @pl.when(i == slot_d)
@@ -529,8 +542,8 @@
         def _():
             finish(b - 1)
 
-        for stage in range(5):
-            r = f - CH - 2 * stage
+        for stage, after in enumerate((0, 2, 4, 5, 6)):
+            r = f - CH - after
 
             @pl.when((r >= 0) & (r < GROUPS * CH) & (lax.rem(r, CH) == 0))
             def _():
@@ -561,9 +574,9 @@
         return carried
 
     def skip_sum(axis):
+        sk_all(axis).wait_recv()
         total = sk[axis, 0]
         for n in sk_range(axis):
-            sk_copy(axis, n).wait_recv()
             total = total + sk[axis, n]
         if axis < 3:
             sk[axis + 1, 0] = total
@@ -679,53 +692,35 @@
     dlog = jnp.dot(turned_acc, tri, precision=HIGHEST, preferred_element_type=F32)
     dlog_ref[...] = dlog[:HEADS]
     total = red[s, z, y].astype(F32)
-    for n in range(1, 4):
-        x_copy(n).wait_recv()
+    x_all().wait_recv()
     for n in range(3):
         total = total + xr[n].astype(F32)
     fin[c, s] = total.astype(BF)
     for n, other in spread:
         a_copy(n, other).start()
-    for n, other in spread:
-        a_copy(n, other).wait_recv()
-
-    def drain(k, carried):
-        put_x(k).wait()
-
-        @pl.when(s < 3)
-        def _():
-            fwd(k).wait_send()
-
-        @pl.when(s > 0)
-        def _():
-            bwd(k).wait_send()
-
-        return carried
-
-    lax.fori_loop(0, K, drain, 0)
-
-    def drain_groups(g, _):
-        cg_copy(g).wait_send()
-        for p in range(2):
-            for stage in range(4):
-                for d in range(2):
-                    r_copy(g, p, stage, d).wait_send()
-        return _
-
-    lax.fori_loop(0, GROUPS, drain_groups, 0)
-    for q in range(4):
-        cp_copy(q).wait_send()
-        for p in range(2):
-            for stage in range(4):
-                for d in range(2):
-                    w_copy(q, p, stage, d).wait_send()
-    for n in range(1, 4):
-        x_copy(n).wait_send()
-    for n, other in spread:
-        a_copy(n, other).wait_send()
+    a_all(0).wait_recv()
+    a_all(1).wait_recv()
+
+    pltpu.make_async_copy(gs, gs, store_x).wait()
+
+    @pl.when(s < 3)
+    def _():
+        remote(eout, er, f_send, f_recv.at[0], sibling).wait_send()
+
+    @pl.when(s > 0)
+    def _():
+        remote(adj, lr, b_send, b_recv.at[0], sibling).wait_send()
+
+    for stage in range(4):
+        w_sent(stage)
+        r_sent(stage)
+    remote(cp_send, cp_recv, cp_ssem, cp_rsem.at[0], sibling).wait_send()
+    remote(cg.at[0], cg.at[1], cg_send, cg_recv.at[0], sibling).wait_send()
+    x_all().wait_send()
+    a_all(0).wait_send()
+    a_all(1).wait_send()
     for axis in range(4):
-        for n in sk_range(axis):
-            sk_copy(axis, n).wait_send()
+        sk_all(axis).wait_send()
 
 
 def publish(
@@ -819,27 +814,27 @@
             dma((K,)),
             dma,
             dma((4,)),
+            dma,
+            dma,
+            dma,
+            dma((4,)),
+            dma((4, 4)),
+            dma,
             dma((K,)),
             dma,
-            dma,
-            dma((4, 2, 4, 2)),
-            dma((4, 2, 4, 2)),
             dma((K,)),
-            dma((K,)),
-            dma((K,)),
-            dma((K,)),
+            dma,
+            dma((4,)),
+            dma,
+            dma((GROUPS,)),
+            dma((4,)),
+            dma((GROUPS, 4)),
+            dma,
+            dma,
+            dma((2,)),
+            dma((2,)),
             dma((4,)),
             dma((4,)),
-            dma((GROUPS,)),
-            dma((GROUPS,)),
-            dma((GROUPS, 2, 4, 2)),
-            dma((GROUPS, 2, 4, 2)),
-            dma((4,)),
-            dma((4,)),
-            dma((4, 2)),
-            dma((4, 2)),
-            dma((4, 4)),
-            dma((4, 4)),
         ],
         compiler_params=pltpu.CompilerParams(
             collective_id=0, has_side_effects=True, vmem_limit_bytes=62 * 1024 * 1024

time: 119 us -> 123 us (1.034)
  Pallas kernels: 118 us -> 122 us
    pallas_call x1, Pallas kernels: 113 us -> 117 us  [on_device(): pl.pallas_call(kernel, out_shape=(jax.ShapeDtypeStruct((TOK, DIM), BF), j...]
where the time goes in v3:
time: 123 us
  Pallas kernels  122 us (99%)
    pallas_call x1, Pallas kernels, on_device(): pl.pallas_call(kernel, out_shape=(jax.ShapeDtypeStruct((TOK, DIM), BF), j...  117 us
    pallas_call x1, Pallas kernels, on_device(): pl.pallas_call(publish, out_shape=(jax.ShapeDtypeStruct((TOK, DIM), BF),...  4.97 us

profile of v3, /device:TPU:1, one launch (start us, length us, event | category | flops | bytes accessed | tf_op | source)
XLA Modules:
  0.0 122.9 jit_solution(7172026985731482681)
XLA Ops:
  0.6 117.3 %shard_map.110 = (bf16[256,8192]{1,0:T(8,128)(2,1)}, bf16[256,512]{1,0:T(8,128)(2,1)}, bf16[2,4,128,256]{3,2,1,0:T(8,128)(2,1)}, f32[64,256]{1,0:T(8,128)}, f32[1,64]{1,0:T(1,128)}) custom-call(bf16[256,8192]{1,0:T(8,128)(2,1)} %bitcast.10, bf16[512,512]{1,0:T(8,128)(2,1)} %cw_hbm.1, bf16[256,8192]{1,0:T(8,128)(2,1)} %bitcast.11, bf16[256,512]{1,0:T(8,128)(2,1)} %bitcast.13, ...), custom_call_target="tpu_custom_call" | custom-call | tf_op jit(solution)/shard_map/pallas_call | solution.py:765
  118.0 5.0 %shard_map.111 = (bf16[256,8192]{1,0:T(8,128)(2,1)}, f32[512,512]{1,0:T(8,128)}, bf16[256,512]{1,0:T(8,128)(2,1)}, f32[64,256]{1,0:T(8,128)}, f32[1,64]{1,0:T(1,128)}) custom-call(bf16[256,8192]{1,0:T(8,128)(2,1)} %get-tuple-element.15.dx_in, bf16[2,4,128,256]{3,2,1,0:T(8,128)(2,1)} %get-tuple-element.16.fin_in, bf16[256,512]{1,0:T(8,128)(2,1)} %get-tuple-element.17.db_in, ...), custom_call_target="tpu_custom_call" | custom-call | tf_op jit(solution)/shard_map/pallas_call | solution.py:851
